TPU v7x, 32 devices: a whole 2x2x4 slice. The times are simulated.
32 devices in a mesh: seq: 16 (over z, y, core), tp: 2 (over x).
Axes of the slice: x: 2, y: 2, z: 4, core: 2. Of those that a mesh axis runs over, the one named last changes fastest.
Arguments:
- queries: bfloat16 [2048, 1024], P('seq'), may hold values from -8 to 8
- key_rows: bfloat16 [2048, 256], P(('seq', 'tp')), may hold values from -4 to 4
- value_rows: bfloat16 [2048, 256], P(('seq', 'tp')), may hold values from -6 to 6
- ssm_input: bfloat16 [2048, 3072], P('seq', 'tp'), may hold values from -0.29882812 to 0.29882812
- gate_input: bfloat16 [2048, 3072], P('seq', 'tp'), may hold values from -6 to 6
- write_vectors: bfloat16 [2048, 256], P('seq'), may hold values from -1.5 to 1.5
- read_vectors: bfloat16 [2048, 256], P('seq'), may hold values from -1.5 to 1.5
- decay_rates: float32 [2048, 48], P('seq', 'tp'), may hold values from 0 to 3, as said below
- attn_out_weight: bfloat16 [1024, 2048], P('tp'), may hold values from -0.8984375 to 0.8984375
- ssm_out_weight: bfloat16 [3072, 2048], P('tp'), may hold values from -0.109375 to 0.109375
Outputs:
- mixer_output: float32 [2048, 2048], P(('seq', 'tp'))
Inputs may be any that keep to these rules, and one draw needn't show every extreme that they name: `decay_rates`: positive.
All inputs are finite; a program needn't handle non-finite values.
Results may differ from a plain program's by a relative error of at most 0.0045.
Values may be sent and summed in bfloat16 or wider, within the bound.
A program may use at most 128 MiB of HBM per device.

v0:
```python
import math

import jax
import jax.numpy as jnp
from jax import lax
from jax.sharding import PartitionSpec as P

ASKER_PROBES = 8
KVHEADS = 2
HEAD = 128


precise = lax.Precision.HIGHEST
masked_score = -1e30


def prefix(value, axis, join, neutral):
    count, mine = (lax.axis_size(axis), lax.axis_index(axis))
    pieces = jax.tree.map(lambda part: lax.all_gather(part, axis), value)
    so_far = jax.tree.map(
        lambda part, zero: jnp.full_like(part, 0) + jnp.asarray(zero, part.dtype), value, neutral
    )

    def turn(position, so_far):
        longer = join(so_far, jax.tree.map(lambda part: part[position], pieces))
        return jax.tree.map(lambda new, old: jnp.where(position < mine, new, old), longer, so_far)

    return lax.fori_loop(0, count - 1, turn, so_far)


def combined_all(value, axis, join):
    pieces = jax.tree.map(lambda part: lax.all_gather(part, axis), value)
    head = jax.tree.map(lambda part: part[0], pieces)
    tail = jax.tree.map(lambda part: part[1:], pieces)
    so_far, _ = lax.scan(lambda so_far, slab: (join(so_far, slab), None), head, tail)
    return so_far


def local_states(ssm_input, write_vectors, read_vectors, decay_rates):
    local_rows = ssm_input.shape[0]
    heads_here = decay_rates.shape[1]
    values_f32 = ssm_input.astype(jnp.float32).reshape(local_rows, heads_here, -1)
    write_f32 = write_vectors.astype(jnp.float32)
    read_f32 = read_vectors.astype(jnp.float32)
    decay_sum = jnp.cumsum(-decay_rates, axis=0)
    block_decay = decay_sum[-1]
    positions = jnp.arange(local_rows)
    causal = (positions[:, None] >= positions[None, :])[:, :, None]
    decay_gap = jnp.where(causal, decay_sum[:, None, :] - decay_sum[None, :, :], 0.0)
    read_write = jnp.dot(read_vectors, write_vectors.T, preferred_element_type=jnp.float32)
    factor = jnp.where(causal, jnp.exp(decay_gap), 0.0) * read_write[:, :, None]
    within = jnp.einsum("tsh,shp->thp", factor, values_f32, precision=precise)
    block_state = jnp.einsum(
        "sh,shp,sn->hpn",
        jnp.exp(block_decay[None, :] - decay_sum),
        values_f32,
        write_f32,
        precision=precise,
    )
    return (within, block_state, decay_sum, read_f32)


def combine_states(earlier, later):
    return (earlier[0] * later[0], later[0][:, None, None] * earlier[1] + later[1])


def join_partial(first_part, second_part):
    updated_peak = jnp.maximum(first_part[0], second_part[0])
    first_scale = jnp.exp(first_part[0] - updated_peak)
    second_scale = jnp.exp(second_part[0] - updated_peak)
    running_sum = first_part[1] * first_scale + second_part[1] * second_scale
    weighted = first_part[2] * first_scale[..., None] + second_part[2] * second_scale[..., None]
    return (updated_peak, running_sum, weighted)


def local(
    queries,
    key_rows,
    value_rows,
    ssm_input,
    gate_input,
    write_vectors,
    read_vectors,
    decay_rates,
    attn_out_weight,
    ssm_out_weight,
):
    local_rows = queries.shape[0]
    within, block_state, decay_sum, read_f32 = local_states(
        ssm_input, write_vectors, read_vectors, decay_rates
    )
    block_decay = jnp.exp(decay_sum[-1])
    neutral = (jnp.ones_like(block_decay), jnp.zeros_like(block_state))
    entering = prefix((block_decay, block_state), "seq", combine_states, neutral)
    carried = jnp.einsum(
        "th,tn,hpn->thp", jnp.exp(decay_sum), read_f32, entering[1], precision=precise
    )
    ssm_raw = (within + carried).reshape(local_rows, -1)
    ssm_half = (ssm_raw * jax.nn.silu(gate_input.astype(jnp.float32))).astype(jnp.bfloat16)
    group = ASKER_PROBES // KVHEADS
    query_heads = queries.reshape(local_rows, KVHEADS, group, HEAD)
    slice_rows = key_rows.shape[0]
    seq_index = lax.axis_index("seq")
    tp_index = lax.axis_index("tp")
    query_place = seq_index * local_rows + jnp.arange(local_rows)
    score_scale = 1.0 / math.sqrt(HEAD)
    start_max = jnp.full((local_rows, KVHEADS, group), masked_score, jnp.float32)
    start_sum = jnp.zeros((local_rows, KVHEADS, group), jnp.float32)
    start_weighted = jnp.zeros((local_rows, KVHEADS, group, HEAD), jnp.float32)
    running = (start_max, start_sum, start_weighted)
    first_row = jnp.int32(0)
    key_segment = lax.all_gather(key_rows, "seq", axis=0, tiled=True)
    value_part = lax.all_gather(value_rows, "seq", axis=0, tiled=True)
    piece_rows = key_segment.shape[0]
    for lower_row in range(0, piece_rows, 256):
        upper_row = min(lower_row + 256, piece_rows)
        attend_key_segment = key_segment[lower_row:upper_row]
        attend_value_part = value_part[lower_row:upper_row]
        attend_first_row = first_row + lower_row
        attend_piece_rows = attend_key_segment.shape[0]
        row_ids = attend_first_row + jnp.arange(attend_piece_rows)
        key_place = (
            row_ids // slice_rows * local_rows + tp_index * slice_rows + row_ids % slice_rows
        )
        compute_running_max, compute_running_sum, compute_weighted = running
        key_block = attend_key_segment.reshape(attend_piece_rows, KVHEADS, HEAD)
        value_block = attend_value_part.reshape(attend_piece_rows, KVHEADS, HEAD)
        scores = (
            jnp.einsum("tgqd,ngd->tgqn", query_heads, key_block, preferred_element_type=jnp.float32)
            * score_scale
        )
        visible = (key_place[None, :] <= query_place[:, None])[:, None, None, :]
        scores = jnp.where(visible, scores, masked_score)
        updated_peak = jnp.maximum(compute_running_max, jnp.max(scores, axis=-1))
        weights = jnp.where(visible, jnp.exp(scores - updated_peak[..., None]), 0.0)
        factor = jnp.exp(compute_running_max - updated_peak)
        compute_running_sum = compute_running_sum * factor + jnp.sum(weights, axis=-1)
        compute_weighted = compute_weighted * factor[..., None] + jnp.einsum(
            "tgqn,ngd->tgqd",
            weights.astype(jnp.bfloat16),
            value_block,
            preferred_element_type=jnp.float32,
        )
        running = (updated_peak, compute_running_sum, compute_weighted)
    running_max, running_sum, weighted = running
    heads_mine = ASKER_PROBES // lax.axis_size("tp")
    running_max, running_sum, weighted = combined_all(
        (running_max, running_sum, weighted), "tp", join_partial
    )
    all_heads = (weighted / running_sum[..., None]).reshape(local_rows, ASKER_PROBES, HEAD)
    own_heads = lax.dynamic_slice_in_dim(all_heads, tp_index * heads_mine, heads_mine, 1)
    attn_half = own_heads.reshape(local_rows, heads_mine * HEAD).astype(jnp.bfloat16)
    attention_share = lax.psum_scatter(
        jnp.dot(attn_half, attn_out_weight, preferred_element_type=jnp.float32),
        "tp",
        scatter_dimension=0,
        tiled=True,
    )
    state_share = lax.psum_scatter(
        jnp.dot(ssm_half, ssm_out_weight, preferred_element_type=jnp.float32),
        "tp",
        scatter_dimension=0,
        tiled=True,
    )
    summed = attention_share + state_share
    return summed


def solution(mesh):
    placed = (
        P("seq", None),
        P(("seq", "tp"), None),
        P(("seq", "tp"), None),
        P("seq", "tp"),
        P("seq", "tp"),
        P("seq", None),
        P("seq", None),
        P("seq", "tp"),
        P("tp", None),
        P("tp", None),
    )
    return jax.shard_map(
        local, mesh=mesh, in_specs=placed, out_specs=P(("seq", "tp"), None), check_vma=False
    )
```

profile of v0, /device:TPU:24, one launch (start us, length us, event | category | flops | bytes accessed | tf_op | source)
XLA Modules:
  0.0 308.1 jit_solution(4127619843116148237)
XLA Ops:
  6.6 18.6 %all_gather.30 = bf16[1024,256]{1,0:T(8,128)(2,1)S(1)} all-gather(bf16[64,256]{1,0:T(8,128)(2,1)} %param.13), channel_id=1, replica_groups=mesh['seq'=16,'tp'=2] {'seq'}, dimensions={0}, use_global_device_ids=true | all-gather | bytes 557056 | tf_op jit(solution)/shard_map/all_gather | solution.py:112
  28.5 19.6 %all_gather.31 = bf16[1024,256]{1,0:T(8,128)(2,1)S(1)} all-gather(bf16[64,256]{1,0:T(8,128)(2,1)S(1)} %copy-done.30), channel_id=1, replica_groups=mesh['seq'=16,'tp'=2] {'seq'}, dimensions={0}, use_global_device_ids=true | all-gather | bytes 557056 | tf_op jit(solution)/shard_map/all_gather | solution.py:113
  56.3 1.7 fusion.26
  61.5 2.8 fusion.39
  64.3 1.5 copy.81
  65.8 1.5 copy.84
  67.4 19.0 %all-gather.2 = f32[16,1,24]{2,1,0:T(1,128)} all-gather(f32[1,1,24]{2,1,0:T(1,128)} %get-tuple-element.171), channel_id=1, replica_groups=mesh['seq'=16,'tp'=2] {'seq'}, dimensions={0}, use_global_device_ids=true | all-gather | bytes 1632 | tf_op jit(solution)/shard_map/all_gather | solution.py:19
  87.9 1.5 fusion.31
  89.9 4.3 %all_gather.34 = f32[2,128,2,4]{1,3,2,0:T(4,128)S(1)} all-gather(f32[1,128,2,4]{1,3,2,0:T(4,128)S(1)} %get-tuple-element.172), channel_id=1, replica_groups=mesh['seq'=16,'tp'=2] {'tp'}, dimensions={0}, use_global_device_ids=true | all-gather | bytes 12288 | tf_op jit(solution)/shard_map/all_gather | solution.py:32
  94.2 4.3 %all_gather.35 = f32[2,128,2,4]{1,3,2,0:T(4,128)S(1)} all-gather(f32[1,128,2,4]{1,3,2,0:T(4,128)S(1)} %get-tuple-element.173), channel_id=1, replica_groups=mesh['seq'=16,'tp'=2] {'tp'}, dimensions={0}, use_global_device_ids=true | all-gather | bytes 12288 | tf_op jit(solution)/shard_map/all_gather | solution.py:32
  98.8 2.9 fusion.15
  103.4 108.6 %all-gather.8.cloned.1.call-done = f32[384,64,256]{2,1,0:T(8,128)} async-done(((f32[24,64,256]{2,1,0:T(8,128)}), f32[384,64,256]{2,1,0:T(8,128)}) %all-gather.8.cloned.1.call-update) | async-done | bytes 25165840 | tf_op jit(solution)/shard_map/all_gather | solution.py:19
  212.0 59.8 %while.9 = (s32[]{:T(128)}, f32[24,64,256]{2,1,0:T(8,128)}, s32[]{:T(128)}, f32[16,24]{1,0:T(8,128)}, f32[16,24,64,256]{3,2,1,0:T(8,128)}, /*index=5*/s32[]{:T(128)}, s32[]{:T(128)}) while((s32[]{:T(128)}, f32[24,64,256]{2,1,0:T(8,128)}, s32[]{:T(128)}, f32[16,24]{1,0:T(8,128)}, f32[16,24,64,256]{3,2,1,0:T(8,128)}, ...), condition=%wide.region_11.12_spmd.clone, body=%wide.region_10.11_spmd.clone.sunk | while | flops 1572868 | bytes 4718985 | solution.py:28
  212.7 2.9 fusion.127
  216.2 3.3 %fusion.127 = f32[24,64,256]{2,1,0:T(8,128)} fusion(f32[16,24,64,256]{3,2,1,0:T(8,128)} %get-tuple-element.249, s32[]{:T(128)} %get-tuple-element.238, f32[24,64,256]{2,1,0:T(8,128)} %get-tuple-element.239, f32[24]{0:T(128)S(1)} %dynamic-slice_bitcast_fusion.2, pred[]{:T(512)S(6)} %compare.41, pred[]{:T(512)S(6)} %lt.61), kind=kLoop, calls=%fused_computation.1.clone.1 | loop fusion | flops 1572864 | bytes 4718694 | tf_op jit(solution)/shard_map/while/body/eval_jaxpr/jit(_where)/select_n | solution.py:26
  220.2 3.3 %fusion.127 = f32[24,64,256]{2,1,0:T(8,128)} fusion(f32[16,24,64,256]{3,2,1,0:T(8,128)} %get-tuple-element.249, s32[]{:T(128)} %get-tuple-element.238, f32[24,64,256]{2,1,0:T(8,128)} %get-tuple-element.239, f32[24]{0:T(128)S(1)} %dynamic-slice_bitcast_fusion.2, pred[]{:T(512)S(6)} %compare.41, pred[]{:T(512)S(6)} %lt.61), kind=kLoop, calls=%fused_computation.1.clone.1 | loop fusion | flops 1572864 | bytes 4718694 | tf_op jit(solution)/shard_map/while/body/eval_jaxpr/jit(_where)/select_n | solution.py:26
  224.3 3.3 %fusion.127 = f32[24,64,256]{2,1,0:T(8,128)} fusion(f32[16,24,64,256]{3,2,1,0:T(8,128)} %get-tuple-element.249, s32[]{:T(128)} %get-tuple-element.238, f32[24,64,256]{2,1,0:T(8,128)} %get-tuple-element.239, f32[24]{0:T(128)S(1)} %dynamic-slice_bitcast_fusion.2, pred[]{:T(512)S(6)} %compare.41, pred[]{:T(512)S(6)} %lt.61), kind=kLoop, calls=%fused_computation.1.clone.1 | loop fusion | flops 1572864 | bytes 4718694 | tf_op jit(solution)/shard_map/while/body/eval_jaxpr/jit(_where)/select_n | solution.py:26
  228.3 3.3 %fusion.127 = f32[24,64,256]{2,1,0:T(8,128)} fusion(f32[16,24,64,256]{3,2,1,0:T(8,128)} %get-tuple-element.249, s32[]{:T(128)} %get-tuple-element.238, f32[24,64,256]{2,1,0:T(8,128)} %get-tuple-element.239, f32[24]{0:T(128)S(1)} %dynamic-slice_bitcast_fusion.2, pred[]{:T(512)S(6)} %compare.41, pred[]{:T(512)S(6)} %lt.61), kind=kLoop, calls=%fused_computation.1.clone.1 | loop fusion | flops 1572864 | bytes 4718694 | tf_op jit(solution)/shard_map/while/body/eval_jaxpr/jit(_where)/select_n | solution.py:26
  232.3 3.4 %fusion.127 = f32[24,64,256]{2,1,0:T(8,128)} fusion(f32[16,24,64,256]{3,2,1,0:T(8,128)} %get-tuple-element.249, s32[]{:T(128)} %get-tuple-element.238, f32[24,64,256]{2,1,0:T(8,128)} %get-tuple-element.239, f32[24]{0:T(128)S(1)} %dynamic-slice_bitcast_fusion.2, pred[]{:T(512)S(6)} %compare.41, pred[]{:T(512)S(6)} %lt.61), kind=kLoop, calls=%fused_computation.1.clone.1 | loop fusion | flops 1572864 | bytes 4718694 | tf_op jit(solution)/shard_map/while/body/eval_jaxpr/jit(_where)/select_n | solution.py:26
  236.3 3.3 %fusion.127 = f32[24,64,256]{2,1,0:T(8,128)} fusion(f32[16,24,64,256]{3,2,1,0:T(8,128)} %get-tuple-element.249, s32[]{:T(128)} %get-tuple-element.238, f32[24,64,256]{2,1,0:T(8,128)} %get-tuple-element.239, f32[24]{0:T(128)S(1)} %dynamic-slice_bitcast_fusion.2, pred[]{:T(512)S(6)} %compare.41, pred[]{:T(512)S(6)} %lt.61), kind=kLoop, calls=%fused_computation.1.clone.1 | loop fusion | flops 1572864 | bytes 4718694 | tf_op jit(solution)/shard_map/while/body/eval_jaxpr/jit(_where)/select_n | solution.py:26
  240.3 3.3 %fusion.127 = f32[24,64,256]{2,1,0:T(8,128)} fusion(f32[16,24,64,256]{3,2,1,0:T(8,128)} %get-tuple-element.249, s32[]{:T(128)} %get-tuple-element.238, f32[24,64,256]{2,1,0:T(8,128)} %get-tuple-element.239, f32[24]{0:T(128)S(1)} %dynamic-slice_bitcast_fusion.2, pred[]{:T(512)S(6)} %compare.41, pred[]{:T(512)S(6)} %lt.61), kind=kLoop, calls=%fused_computation.1.clone.1 | loop fusion | flops 1572864 | bytes 4718694 | tf_op jit(solution)/shard_map/while/body/eval_jaxpr/jit(_where)/select_n | solution.py:26
  244.3 3.3 %fusion.127 = f32[24,64,256]{2,1,0:T(8,128)} fusion(f32[16,24,64,256]{3,2,1,0:T(8,128)} %get-tuple-element.249, s32[]{:T(128)} %get-tuple-element.238, f32[24,64,256]{2,1,0:T(8,128)} %get-tuple-element.239, f32[24]{0:T(128)S(1)} %dynamic-slice_bitcast_fusion.2, pred[]{:T(512)S(6)} %compare.41, pred[]{:T(512)S(6)} %lt.61), kind=kLoop, calls=%fused_computation.1.clone.1 | loop fusion | flops 1572864 | bytes 4718694 | tf_op jit(solution)/shard_map/while/body/eval_jaxpr/jit(_where)/select_n | solution.py:26
  248.4 3.3 %fusion.127 = f32[24,64,256]{2,1,0:T(8,128)} fusion(f32[16,24,64,256]{3,2,1,0:T(8,128)} %get-tuple-element.249, s32[]{:T(128)} %get-tuple-element.238, f32[24,64,256]{2,1,0:T(8,128)} %get-tuple-element.239, f32[24]{0:T(128)S(1)} %dynamic-slice_bitcast_fusion.2, pred[]{:T(512)S(6)} %compare.41, pred[]{:T(512)S(6)} %lt.61), kind=kLoop, calls=%fused_computation.1.clone.1 | loop fusion | flops 1572864 | bytes 4718694 | tf_op jit(solution)/shard_map/while/body/eval_jaxpr/jit(_where)/select_n | solution.py:26
  252.4 3.3 %fusion.127 = f32[24,64,256]{2,1,0:T(8,128)} fusion(f32[16,24,64,256]{3,2,1,0:T(8,128)} %get-tuple-element.249, s32[]{:T(128)} %get-tuple-element.238, f32[24,64,256]{2,1,0:T(8,128)} %get-tuple-element.239, f32[24]{0:T(128)S(1)} %dynamic-slice_bitcast_fusion.2, pred[]{:T(512)S(6)} %compare.41, pred[]{:T(512)S(6)} %lt.61), kind=kLoop, calls=%fused_computation.1.clone.1 | loop fusion | flops 1572864 | bytes 4718694 | tf_op jit(solution)/shard_map/while/body/eval_jaxpr/jit(_where)/select_n | solution.py:26
  256.4 3.3 %fusion.127 = f32[24,64,256]{2,1,0:T(8,128)} fusion(f32[16,24,64,256]{3,2,1,0:T(8,128)} %get-tuple-element.249, s32[]{:T(128)} %get-tuple-element.238, f32[24,64,256]{2,1,0:T(8,128)} %get-tuple-element.239, f32[24]{0:T(128)S(1)} %dynamic-slice_bitcast_fusion.2, pred[]{:T(512)S(6)} %compare.41, pred[]{:T(512)S(6)} %lt.61), kind=kLoop, calls=%fused_computation.1.clone.1 | loop fusion | flops 1572864 | bytes 4718694 | tf_op jit(solution)/shard_map/while/body/eval_jaxpr/jit(_where)/select_n | solution.py:26
  260.4 3.3 %fusion.127 = f32[24,64,256]{2,1,0:T(8,128)} fusion(f32[16,24,64,256]{3,2,1,0:T(8,128)} %get-tuple-element.249, s32[]{:T(128)} %get-tuple-element.238, f32[24,64,256]{2,1,0:T(8,128)} %get-tuple-element.239, f32[24]{0:T(128)S(1)} %dynamic-slice_bitcast_fusion.2, pred[]{:T(512)S(6)} %compare.41, pred[]{:T(512)S(6)} %lt.61), kind=kLoop, calls=%fused_computation.1.clone.1 | loop fusion | flops 1572864 | bytes 4718694 | tf_op jit(solution)/shard_map/while/body/eval_jaxpr/jit(_where)/select_n | solution.py:26
  264.4 3.3 %fusion.127 = f32[24,64,256]{2,1,0:T(8,128)} fusion(f32[16,24,64,256]{3,2,1,0:T(8,128)} %get-tuple-element.249, s32[]{:T(128)} %get-tuple-element.238, f32[24,64,256]{2,1,0:T(8,128)} %get-tuple-element.239, f32[24]{0:T(128)S(1)} %dynamic-slice_bitcast_fusion.2, pred[]{:T(512)S(6)} %compare.41, pred[]{:T(512)S(6)} %lt.61), kind=kLoop, calls=%fused_computation.1.clone.1 | loop fusion | flops 1572864 | bytes 4718694 | tf_op jit(solution)/shard_map/while/body/eval_jaxpr/jit(_where)/select_n | solution.py:26
  268.4 3.3 %fusion.127 = f32[24,64,256]{2,1,0:T(8,128)} fusion(f32[16,24,64,256]{3,2,1,0:T(8,128)} %get-tuple-element.249, s32[]{:T(128)} %get-tuple-element.238, f32[24,64,256]{2,1,0:T(8,128)} %get-tuple-element.239, f32[24]{0:T(128)S(1)} %dynamic-slice_bitcast_fusion.2, pred[]{:T(512)S(6)} %compare.41, pred[]{:T(512)S(6)} %lt.61), kind=kLoop, calls=%fused_computation.1.clone.1 | loop fusion | flops 1572864 | bytes 4718694 | tf_op jit(solution)/shard_map/while/body/eval_jaxpr/jit(_where)/select_n | solution.py:26
  271.8 2.4 fusion.19
  275.4 4.2 %fusion.64 = f32[128,2048]{1,0:T(8,128)S(1)} fusion(bf16[1536,2048]{1,0:T(8,128)(2,1)} %param.21, f32[128,1536]{1,0:T(8,128)} %copy.86, bf16[128,1536]{1,0:T(8,128)(2,1)} %param.16), kind=kOutput, calls=%fused_computation.76 | convolution fusion | flops 806682624 | bytes 8519680 | tf_op jit(solution)/shard_map/dot_general | solution.py:160
  279.6 1.5 convolution_add_fusion
  281.1 20.5 %reduce-scatter.2.cloned.1.call-done = f32[64,2048]{1,0:T(8,128)} async-done(((f32[128,2048]{1,0:T(8,128)}), f32[64,2048]{1,0:T(8,128)}) %reduce-scatter.2.cloned.1.call-update) | async-done | bytes 524304 | tf_op jit(solution)/shard_map/reduce_scatter | solution.py:153
  (140 shorter events, 30.0 us)
Async XLA Ops:
  6.5 273.1 %copy-start = (bf16[512,2048]{1,0:T(8,128)(2,1)S(1)}, bf16[512,2048]{1,0:T(8,128)(2,1)}, u32[]{:S(2)}) copy-start(bf16[512,2048]{1,0:T(8,128)(2,1)} %param.20) | copy-start | bytes 6291460
  6.5 19.5 %copy-start.20 = (bf16[128,1024]{1,0:T(8,128)(2,1)S(1)}, bf16[128,1024]{1,0:T(8,128)(2,1)}, u32[]{:S(2)}) copy-start(bf16[128,1024]{1,0:T(8,128)(2,1)} %param.12) | copy-start | bytes 786436
  6.5 95.2 %all-gather.6.cloned.1.call-start = ((), (), s32[]{:S(2)}) async-start(), calls=%async_computation.1 | async-start | bytes 1572864 | tf_op jit(solution)/shard_map/all_gather | solution.py:32
  6.6 21.9 %copy-start.30 = (bf16[64,256]{1,0:T(8,128)(2,1)S(1)}, bf16[64,256]{1,0:T(8,128)(2,1)}, u32[]{:S(2)}) copy-start(bf16[64,256]{1,0:T(8,128)(2,1)} %param.14) | copy-start | bytes 98308
  50.5 2.9 copy-start.9
  50.7 4.1 %copy-start.12 = (pred[128,256]{0,1:T(8,128)(4,1)}, pred[128,256]{0,1:T(8,128)(4,1)S(1)}, u32[]{:S(2)}) copy-start(pred[128,256]{0,1:T(8,128)(4,1)S(1)} %get-tuple-element.180) | copy-start | bytes 98308
  50.7 4.5 %copy-start.10 = (pred[128,256]{0,1:T(8,128)(4,1)}, pred[128,256]{0,1:T(8,128)(4,1)S(1)}, u32[]{:S(2)}) copy-start(pred[128,256]{0,1:T(8,128)(4,1)S(1)} %get-tuple-element.181) | copy-start | bytes 98308
  50.7 5.0 %copy-start.13 = (pred[128,256]{0,1:T(8,128)(4,1)}, pred[128,256]{0,1:T(8,128)(4,1)S(1)}, u32[]{:S(2)}) copy-start(pred[128,256]{0,1:T(8,128)(4,1)S(1)} %get-tuple-element.182) | copy-start | bytes 98308
  50.7 5.5 %copy-start.6 = (pred[128,256]{0,1:T(8,128)(4,1)}, pred[128,256]{0,1:T(8,128)(4,1)S(1)}, u32[]{:S(2)}) copy-start(pred[128,256]{0,1:T(8,128)(4,1)S(1)} %get-tuple-element.183) | copy-start | bytes 98308
  52.0 1.8 copy-start.22
  52.0 2.3 copy-start.8
  53.4 1.9 copy-start.1
  53.4 1.4 copy-start.16
  53.8 1.4 copy-start.3
  54.7 1.0 copy-start.4
  54.8 1.1 copy-start.14
  56.3 1.8 copy-start.32
  58.0 154.0 %all-gather.8.cloned.1.call-start = ((), (), s32[]{:S(2)}) async-start(), calls=%async_computation.2 | async-start | bytes 26738688 | tf_op jit(solution)/shard_map/all_gather | solution.py:19
  58.3 1.3 copy-start.5
  64.3 237.3 %reduce-scatter.2.cloned.1.call-start = ((), (), s32[]{:S(2)}) async-start(), calls=%async_computation.3 | async-start | bytes 1572864 | tf_op jit(solution)/shard_map/reduce_scatter | solution.py:153
  67.4 22.0 %copy-start.2 = (f32[128,2,4,256]{0,3,2,1:T(8,128)S(1)}, f32[128,2,4,256]{0,3,2,1:T(8,128)}, u32[]{:S(2)}) copy-start(f32[128,2,4,256]{0,3,2,1:T(8,128)} %copy-done.1) | copy-start | bytes 3145732
  67.4 22.0 %copy-start.11 = (pred[128,256]{0,1:T(8,128)(4,1)S(1)}, pred[128,256]{0,1:T(8,128)(4,1)}, u32[]{:S(2)}) copy-start(pred[128,256]{0,1:T(8,128)(4,1)} %copy-done.10) | copy-start | bytes 98308
  86.4 3.2 %copy-start.7 = (pred[128,256]{0,1:T(8,128)(4,1)S(1)}, pred[128,256]{0,1:T(8,128)(4,1)}, u32[]{:S(2)}) copy-start(pred[128,256]{0,1:T(8,128)(4,1)} %copy-done.6) | copy-start | bytes 98308
  87.8 2.0 copy-start.23
  87.8 2.0 copy-start.25
  87.9 2.0 copy-start.27
  87.9 2.0 copy-start.29
  87.9 10.8 %copy-start.17 = (bf16[128,256]{1,0:T(8,128)(2,1)S(1)}, bf16[128,256]{1,0:T(8,128)(2,1)}, u32[]{:S(2)}) copy-start(bf16[128,256]{1,0:T(8,128)(2,1)} %param.17) | copy-start | bytes 196612
  87.9 10.8 %copy-start.18 = (bf16[128,256]{1,0:T(8,128)(2,1)S(1)}, bf16[128,256]{1,0:T(8,128)(2,1)}, u32[]{:S(2)}) copy-start(bf16[128,256]{1,0:T(8,128)(2,1)} %param.18) | copy-start | bytes 196612
  87.9 10.9 %copy-start.31 = (f32[128,24]{0,1:T(8,128)S(1)}, f32[128,24]{0,1:T(8,128)}, u32[]{:S(2)}) copy-start(f32[128,24]{0,1:T(8,128)} %copy.81) | copy-start | bytes 36868
  212.0 59.8 %copy-start.19 = (bf16[128,256]{1,0:T(8,128)(2,1)S(1)}, bf16[128,256]{1,0:T(8,128)(2,1)}, u32[]{:S(2)}) copy-start(bf16[128,256]{1,0:T(8,128)(2,1)} %param.18) | copy-start | bytes 196612
  212.0 59.8 %copy-start.21 = (f32[128,24]{0,1:T(8,128)S(1)}, f32[128,24]{0,1:T(8,128)}, u32[]{:S(2)}) copy-start(f32[128,24]{0,1:T(8,128)} %copy.84) | copy-start | bytes 36868
  (4 other events, 3.0 us)
Sparse Core Ops, SparseCore 0:
  58.1 23.6 all-gather.5
  83.3 128.5 all-gather.7
  281.2 20.3 reduce-scatter.1
where the time goes:
time: 311 us; the launch traced here: 308 us
  waiting for transfers between devices  129 us (41%)
  blocking collectives  65.9 us (21%)
  other arithmetic  54 us (17%)
  local copies, waits for them, and re-layouts  25.3 us (8%)
  matrix products  20 us (6%)
  between operations  13.7 us (4%)
    all_gather x1, waiting for transfers between devices, prefix(): pieces = jax.tree.map(lambda part: lax.all_gather(part, axis), value)  109 us
    select_n x15, other arithmetic, turn(): jnp.where(position < mine, new, old)  49.5 us
    reduce_scatter x1, waiting for transfers between devices, local(): lax.psum_scatter(jnp.dot(attn_half, attn_out_weight, preferred_element_ty...  20.5 us
    all_gather x1, blocking collectives, local(): value_part = lax.all_gather(value_rows, 'seq', axis=0, tiled=True)  19.6 us
    all_gather x1, blocking collectives, prefix(): pieces = jax.tree.map(lambda part: lax.all_gather(part, axis), value)  19 us
    all_gather x1, blocking collectives, local(): key_segment = lax.all_gather(key_rows, 'seq', axis=0, tiled=True)  18.6 us
    mul x15, local copies, waits for them, and re-layouts, combine_states(): later[0][:, None, None] * earlier[1] + later[1]  10.2 us
    all_gather x2, blocking collectives, combined_all(): pieces = jax.tree.map(lambda part: lax.all_gather(part, axis), value)  8.67 us
  transfers between devices with their start and end apart: 3, of which 2 were waited for; matrix products, arithmetic and copies ran while one was open for 6% of the time, Pallas kernels for 0%

commit v1 on v0

v1 whole, which is shorter than its diff:
```python
import functools
import math

import jax
import jax.numpy as jnp
from jax import lax
from jax.experimental import pallas as pl
from jax.experimental.pallas import tpu as pltpu
from jax.sharding import PartitionSpec as P

KVHEADS = 2
HEAD = 128
HDIM = 64
PLANE = 4
MESH = pl.DeviceIdType.MESH
F32 = jnp.float32
BF16 = jnp.bfloat16
PRECISE = lax.Precision.HIGHEST


def dot(a, b):
    return jnp.dot(a, b, preferred_element_type=F32)


def dot_tn(a, b, precision=None):
    dims = (((0,), (0,)), ((), ()))
    return lax.dot_general(a, b, dims, precision=precision, preferred_element_type=F32)


def dot_nt(a, b):
    dims = (((1,), (1,)), ((), ()))
    return lax.dot_general(a, b, dims, preferred_element_type=F32)


def quarter_starts(width):
    span = -(-width // (PLANE * 128)) * 128
    return span, [min(q * span, width - span) for q in range(PLANE)]


def kernel(
    n, tp, heads, nq,
    q_ref, k_ref, v_ref, x_ref, gate_ref, b_ref, c_ref, rate_ref, wa_hbm, ws_hbm,
    out_ref,
    wa, ws, kv, bc, xs, xr, ds, dr, loc, tot, er, es, ysend, yrecv, psend, precv,
    qs, attn, yacc, grow, part, ssm, acc, peak, norm,
    wsem, swap_s, swap_r, col_s, col_r, pl_s, pl_r, bc_s, bc_r, x_s, x_r, d_s, d_r,
    e_s, e_r, y_s, y_r, p_s, p_r,
):
    s = lax.axis_index("seq")
    t = lax.axis_index("tp")
    planes = n // PLANE
    z = s // PLANE
    i = s % PLANE
    rows = q_ref.shape[0]
    width = x_ref.shape[1]
    model = wa.shape[1]
    own = rows // tp
    span, starts = quarter_starts(width)
    nch = span // 128
    ncol = psend.shape[0]
    cols = model // ncol

    def copy(src, dst, send, recv, to):
        return pltpu.make_async_remote_copy(
            src_ref=src, dst_ref=dst, send_sem=send, recv_sem=recv,
            device_id=to, device_id_type=MESH,
        )

    w_copies = [
        pltpu.make_async_copy(wa_hbm, wa, wsem.at[0]),
        pltpu.make_async_copy(ws_hbm, ws, wsem.at[1]),
    ]
    for w in w_copies:
        w.start()

    plane_peers = [z * PLANE + (i + d) % PLANE for d in range(1, PLANE)]
    plane_index = [(i + d) % PLANE for d in range(1, PLANE)]
    tp_peers = [(t + d) % tp for d in range(1, tp)]
    col_peers = [((z + d) % planes) * PLANE + i for d in range(1, planes)]

    barrier = pltpu.get_barrier_semaphore()
    for p in plane_peers + col_peers:
        pl.semaphore_signal(barrier, inc=1, device_id=(p, t), device_id_type=MESH)
    for p in tp_peers:
        pl.semaphore_signal(barrier, inc=1, device_id=(s, p), device_id_type=MESH)
    pl.semaphore_wait(barrier, len(plane_peers) + len(col_peers) + len(tp_peers))

    def kv_cols(peer):
        return pl.ds(pl.multiple_of(peer * KVHEADS // tp * HEAD, HEAD), HEAD)

    def own_rows(peer):
        return pl.ds(pl.multiple_of(peer * own, own), own)

    swaps = []
    for d, p in enumerate(tp_peers):
        for m, ref in enumerate((k_ref, v_ref)):
            swaps.append(copy(
                ref.at[:, kv_cols(p)], kv.at[s, m, own_rows(t)],
                swap_s.at[m, d], swap_r.at[m, d], (s, p),
            ))
    for c in swaps:
        c.start()
    for m, ref in enumerate((k_ref, v_ref)):
        kv[s, m, own_rows(t), :] = ref[:, kv_cols(t)]

    bc_copies = []
    for d, p in enumerate(plane_peers):
        for m, ref in enumerate((b_ref, c_ref)):
            bc_copies.append(copy(
                ref, bc.at[i, m], bc_s.at[m, d], bc_r.at[m, d], (p, t)
            ))
    for c in bc_copies:
        c.start()
    bc[i, 0] = b_ref[...]
    bc[i, 1] = c_ref[...]

    row_id = lax.broadcasted_iota(jnp.int32, (rows, rows), 0)
    col_id = lax.broadcasted_iota(jnp.int32, (rows, rows), 1)
    causal = row_id >= col_id
    lower = jnp.where(causal, 1.0, 0.0).astype(F32)
    upper = jnp.where(row_id <= col_id, 1.0, 0.0).astype(F32)
    rates = -rate_ref[...]
    cum = jnp.dot(lower, rates, precision=PRECISE, preferred_element_type=F32)
    cum_t = dot_tn(rates, upper, PRECISE)
    last = cum[rows - 1:rows, :]
    to_end = jnp.exp(last - cum)
    from_start = jnp.exp(cum)
    whole_decay = jnp.exp(last)
    first_half = lax.broadcasted_iota(jnp.int32, (rows, 128), 1) < HDIM
    first_half_8 = lax.broadcasted_iota(jnp.int32, (8, 128), 1) < HDIM

    def pair_cols(value, pair):
        a = value[:, 2 * pair:2 * pair + 1]
        b = value[:, 2 * pair + 1:2 * pair + 2]
        mask = first_half if value.shape[0] == rows else first_half_8
        return jnp.where(mask, a, b)

    for q in range(PLANE):
        for c in range(nch):
            lo = starts[q] + 128 * c
            pair = lo // 128
            x = x_ref[:, lo:lo + 128].astype(F32)
            xs[q, :, 128 * c:128 * (c + 1)] = (x * pair_cols(to_end, pair)).astype(BF16)
            ds[q, :, 128 * c:128 * (c + 1)] = pair_cols(whole_decay, pair)

    x_copies = []
    for d, p in enumerate(plane_peers):
        x_copies.append(copy(
            xs.at[plane_index[d]], xr.at[i], x_s.at[d], x_r.at[d], (p, t)
        ))
        x_copies.append(copy(
            ds.at[plane_index[d]], dr.at[i], d_s.at[d], d_r.at[d], (p, t)
        ))
    for c in x_copies:
        c.start()
    xr[i] = xs[i]
    dr[i] = ds[i]

    for c in swaps:
        c.wait_recv()

    def to_plane(block):
        src = kv.at[block * PLANE + i]
        return [
            copy(src, src, pl_s.at[block, d], pl_r.at[block, d], (p, t))
            for d, p in enumerate(plane_peers)
        ]

    def up(zz):
        src = kv.at[s]
        return copy(src, src, col_s.at[zz], col_r.at[z], (zz * PLANE + i, t))

    def col_from(zz):
        src = kv.at[zz * PLANE + i]
        return copy(src, src, col_s.at[zz], col_r.at[zz], (s, t))

    @pl.loop(z + 1, planes)
    def _(zz):
        up(zz).start()

    for c in to_plane(z):
        c.start()

    read_write = dot_nt(c_ref[...], b_ref[...])
    for pair in range(width // 128):
        cc = slice(128 * pair, 128 * (pair + 1))
        factors = []
        for h in (2 * pair, 2 * pair + 1):
            gap = jnp.minimum(cum[:, h:h + 1] - cum_t[h:h + 1, :], 0.0)
            factors.append(jnp.where(causal, jnp.exp(gap) * read_write, 0.0).astype(BF16))
        x = x_ref[:, cc]
        zero = jnp.zeros_like(x)
        stacked = jnp.concatenate(
            [jnp.where(first_half, x, zero), jnp.where(first_half, zero, x)], axis=0
        )
        yacc[:, cc] = dot(jnp.concatenate(factors, axis=1), stacked)
        grow[:, cc] = pair_cols(from_start, pair)

    for c in bc_copies + x_copies:
        c.wait_recv()
    for c in range(nch):
        cc = slice(128 * c, 128 * (c + 1))
        total = jnp.zeros((bc.shape[3], 128), F32)
        decay = jnp.ones((1, 128), F32)
        for j in range(PLANE):
            block = dot_tn(bc[j, 0], xr[j, :, cc])
            loc[j, :, cc] = block
            total = dr[j, 0:1, cc] * total + block
            decay = decay * dr[j, 0:1, cc]
        tot[0, :, cc] = total
        dr[PLANE, :, cc] = jnp.broadcast_to(decay, (8, 128))

    def chain(c):
        to = (jnp.minimum(z + 1, planes - 1) * PLANE + i, t)
        return copy(es.at[c], er.at[c], e_s.at[c], e_r.at[c], to)

    @pl.when(z == 0)
    def _():
        er[...] = jnp.zeros_like(er)

    @pl.loop(0, z)
    def _(zz):
        col_from(zz).wait_recv()
        for c in to_plane(zz):
            c.start()

    for c in range(nch):
        cc = slice(128 * c, 128 * (c + 1))

        @pl.when(z > 0)
        def _():
            chain(c).wait_recv()

        @pl.when(z < planes - 1)
        def _():
            entering = er[c].astype(F32)
            es[c] = (dr[PLANE, 0:1, cc] * entering + tot[0, :, cc]).astype(BF16)
            chain(c).start()

    for c in range(nch):
        cc = slice(128 * c, 128 * (c + 1))
        state = er[c].astype(F32)
        for j in range(PLANE):
            ysend[j, :, cc] = dot(bc[j, 1], state.astype(BF16)).astype(BF16)
            if j < PLANE - 1:
                state = dr[j, 0:1, cc] * state + loc[j, :, cc]
    y_copies = [
        copy(ysend.at[plane_index[d]], yrecv.at[i], y_s.at[d], y_r.at[d], (p, t))
        for d, p in enumerate(plane_peers)
    ]
    for c in y_copies:
        c.start()
    yrecv[i] = ysend[i]

    for h in range(nq):
        lo = pl.multiple_of((t * nq + h) * HEAD, HEAD)
        qs[h * rows:(h + 1) * rows, :] = q_ref[:, pl.ds(lo, HEAD)]
    stack = nq * rows
    acc[...] = jnp.zeros_like(acc)
    norm[...] = jnp.zeros_like(norm)
    peak[...] = jnp.full_like(peak, -1e30)
    scale = 1.0 / math.sqrt(HEAD)
    wide = PLANE * rows

    def attend(zz, masked):
        for c in to_plane(zz):
            c.wait_recv()
        keys = kv[pl.ds(zz * PLANE, PLANE), 0].reshape(wide, HEAD)
        vals = kv[pl.ds(zz * PLANE, PLANE), 1].reshape(wide, HEAD)
        for h in range(nq):
            hh = slice(h * rows, (h + 1) * rows)
            scores = dot_nt(qs[hh, :], keys) * scale
            if masked:
                key_id = lax.broadcasted_iota(jnp.int32, (rows, wide), 1)
                query_id = lax.broadcasted_iota(jnp.int32, (rows, wide), 0) + i * rows
                scores = jnp.where(key_id <= query_id, scores, -1e30)
            old = peak[hh, 0:1]
            new = jnp.maximum(old, jnp.max(scores, axis=1, keepdims=True))
            weights = jnp.exp(scores - new)
            shrink = jnp.exp(old - new)
            norm[hh, 0:1] = norm[hh, 0:1] * shrink + jnp.sum(weights, axis=1, keepdims=True)
            acc[hh, :] = acc[hh, :] * shrink + dot(weights.astype(BF16), vals)
            peak[hh, 0:1] = new

    attend(z, True)

    @pl.loop(0, z)
    def _(zz):
        attend(zz, False)

    for h in range(nq):
        hh = slice(h * rows, (h + 1) * rows)
        attn[:, h * HEAD:(h + 1) * HEAD] = (acc[hh, :] / norm[hh, 0:1]).astype(BF16)
    for w in w_copies:
        w.wait()
    for k in range(ncol):
        cc = slice(k * cols, (k + 1) * cols)
        part[:, cc] = dot(attn[...], wa[:, cc])

    for c in y_copies:
        c.wait_recv()
    for q in range(PLANE):
        for c in range(nch):
            lo = starts[q] + 128 * c
            cc = slice(lo, lo + 128)
            g = gate_ref[:, cc].astype(F32)
            raw = yacc[:, cc] + grow[:, cc] * yrecv[q, :, 128 * c:128 * (c + 1)].astype(F32)
            ssm[:, cc] = (raw * (g / (1.0 + jnp.exp(-g)))).astype(BF16)
    p_copies = []
    for k in range(ncol):
        cc = slice(k * cols, (k + 1) * cols)
        value = part[:, cc] + dot(ssm[...], ws[:, cc])
        part[:, cc] = value
        psend[k] = value.astype(BF16)
        for d, p in enumerate(tp_peers):
            c = copy(
                psend.at[k, own_rows(p)], precv.at[d, k],
                p_s.at[d, k], p_r.at[d, k], (s, p),
            )
            c.start()
            p_copies.append((d, k, c))
    for k in range(ncol):
        cc = slice(k * cols, (k + 1) * cols)
        value = part[own_rows(t), cc]
        for d, kk, c in p_copies:
            if kk == k:
                c.wait_recv()
                value = value + precv[d, k].astype(F32)
        out_ref[:, cc] = value

    for c in swaps + bc_copies + x_copies + y_copies + [c for _, _, c in p_copies]:
        c.wait_send()

    @pl.loop(z + 1, planes)
    def _(zz):
        up(zz).wait_send()

    @pl.loop(0, z + 1)
    def _(zz):
        for c in to_plane(zz):
            c.wait_send()

    @pl.when(z < planes - 1)
    def _():
        for c in range(nch):
            chain(c).wait_send()


def local(
    n, tp,
    queries, key_rows, value_rows, ssm_input, gate_input, write_vectors, read_vectors,
    decay_rates, attn_out_weight, ssm_out_weight,
):
    rows = queries.shape[0]
    width = ssm_input.shape[1]
    heads = decay_rates.shape[1]
    state = write_vectors.shape[1]
    model = attn_out_weight.shape[1]
    nq = queries.shape[1] // HEAD // tp
    planes = n // PLANE
    own = rows // tp
    span, _ = quarter_starts(width)
    nch = span // 128
    ncol = 4
    cols = model // ncol
    peers = PLANE - 1
    vmem = pltpu.VMEM
    dma = pltpu.SemaphoreType.DMA
    return pl.pallas_call(
        functools.partial(kernel, n, tp, heads, nq),
        out_shape=jax.ShapeDtypeStruct((own, model), F32),
        in_specs=[pl.BlockSpec(memory_space=pltpu.VMEM)] * 8
        + [pl.BlockSpec(memory_space=pl.ANY)] * 2,
        out_specs=pl.BlockSpec(memory_space=pltpu.VMEM),
        scratch_shapes=[
            vmem(attn_out_weight.shape, BF16),
            vmem(ssm_out_weight.shape, BF16),
            vmem((n, 2, rows, HEAD), BF16),
            vmem((PLANE, 2, rows, state), BF16),
            vmem((PLANE, rows, span), BF16),
            vmem((PLANE, rows, span), BF16),
            vmem((PLANE, 8, span), F32),
            vmem((PLANE + 1, 8, span), F32),
            vmem((PLANE, state, span), F32),
            vmem((1, state, span), F32),
            vmem((nch, state, 128), BF16),
            vmem((nch, state, 128), BF16),
            vmem((PLANE, rows, span), BF16),
            vmem((PLANE, rows, span), BF16),
            vmem((ncol, rows, cols), BF16),
            vmem((tp - 1, ncol, own, cols), BF16),
            vmem((nq * rows, HEAD), BF16),
            vmem((rows, nq * HEAD), BF16),
            vmem((rows, width), F32),
            vmem((rows, width), F32),
            vmem((rows, model), F32),
            vmem((rows, width), BF16),
            vmem((nq * rows, HEAD), F32),
            vmem((nq * rows, HEAD), F32),
            vmem((nq * rows, HEAD), F32),
            dma((2,)),
            dma((2, tp - 1)),
            dma((2, tp - 1)),
            dma((planes,)),
            dma((planes,)),
            dma((planes, peers)),
            dma((planes, peers)),
            dma((2, peers)),
            dma((2, peers)),
            dma((peers,)),
            dma((peers,)),
            dma((peers,)),
            dma((peers,)),
            dma((nch,)),
            dma((nch,)),
            dma((peers,)),
            dma((peers,)),
            dma((tp - 1, ncol)),
            dma((tp - 1, ncol)),
        ],
        compiler_params=pltpu.CompilerParams(
            collective_id=0, has_side_effects=True, vmem_limit_bytes=56 * 1024 * 1024
        ),
    )(
        queries, key_rows, value_rows, ssm_input, gate_input, write_vectors, read_vectors,
        decay_rates, attn_out_weight, ssm_out_weight,
    )


def solution(mesh):
    placed = (
        P("seq", None),
        P(("seq", "tp"), None),
        P(("seq", "tp"), None),
        P("seq", "tp"),
        P("seq", "tp"),
        P("seq", None),
        P("seq", None),
        P("seq", "tp"),
        P("tp", None),
        P("tp", None),
    )
    body = functools.partial(local, mesh.shape["seq"], mesh.shape["tp"])
    return jax.shard_map(
        body, mesh=mesh, in_specs=placed, out_specs=P(("seq", "tp"), None), check_vma=False
    )
```

time: 311 us -> 48.7 us (0.16)
  waiting for transfers between devices: 129 us -> 0 us
  blocking collectives: 65.9 us -> 0 us
  other arithmetic: 54 us -> 0 us
  Pallas kernels: 0 us -> 45.2 us
  local copies, waits for them, and re-layouts: 25.3 us -> 3.31 us
  matrix products: 20 us -> 0 us
  between operations: 13.7 us -> 0.01 us
    all_gather x2 -> x0, waiting for transfers between devices: 109 us -> none  [the longest x1 109 us: prefix(): pieces = jax.tree.map(lambda part: lax.all_gather(part, axis), value)]
    all_gather x5 -> x0, blocking collectives: 65.9 us -> none  [the longest x1 19.6 us: local(): value_part = lax.all_gather(value_rows, 'seq', axis=0, tiled=True)]
    select_n x15 -> x0, other arithmetic: 49.5 us -> none  [turn(): jnp.where(position < mine, new, old)]
    pallas_call x0 -> x1, Pallas kernels: none -> 45.2 us  [local(): pl.pallas_call(functools.partial(kernel, n, tp, heads, nq), out_shape=jax...]
    reduce_scatter x1 -> x0, waiting for transfers between devices: 20.5 us -> none  [local(): lax.psum_scatter(jnp.dot(attn_half, attn_out_weight, preferred_element_ty...]
    dot_general x14 -> x0, matrix products: 20 us -> none  [the longest x1 4.22 us: local(): jnp.dot(ssm_half, ssm_out_weight, preferred_element_type=jnp.float32)]
    mul x15 -> x0, local copies, waits for them, and re-layouts: 10.2 us -> none  [combine_states(): later[0][:, None, None] * earlier[1] + later[1]]
    unnamed x77 -> x2, local copies, waits for them, and re-layouts: 7.83 us -> 3.31 us
  transfers between devices with their start and end apart: 3 -> 0, of which waited for: 2 -> 0; matrix products, arithmetic and copies ran while one was open for 6% -> 0% of each run, Pallas kernels for 0% -> 0%
where the time goes in v1:
time: 48.7 us; the launch traced here: 48.5 us
  Pallas kernels  45.2 us (93%)
  local copies, waits for them, and re-layouts  3.31 us (7%)
    pallas_call x1, Pallas kernels, local(): pl.pallas_call(functools.partial(kernel, n, tp, heads, nq), out_shape=jax...  45.2 us
    unnamed x2, local copies, waits for them, and re-layouts  3.31 us

profile of v1, /device:TPU:24, one launch (start us, length us, event | category | flops | bytes accessed | tf_op | source)
XLA Modules:
  0.0 48.5 jit_solution(846084356047549666)
XLA Ops:
  0.0 1.4 %copy.11.rate_ref = f32[128,24]{1,0:T(8,128)} copy(f32[128,24]{0,1:T(8,128)} %param.17) | data formatting | bytes 24576 | tf_op args[7]
  1.4 45.2 %shard_map.100 = f32[64,2048]{1,0:T(8,128)} custom-call(bf16[128,1024]{1,0:T(8,128)(2,1)} %q_ref.1, bf16[64,256]{1,0:T(8,128)(2,1)} %k_ref.1, bf16[64,256]{1,0:T(8,128)(2,1)} %v_ref.1, bf16[128,1536]{1,0:T(8,128)(2,1)} %x_ref.1, bf16[128,1536]{1,0:T(8,128)(2,1)} %gate_ref.1, bf16[128,256]{1,0:T(8,128)(2,1)} %b_ref.1, bf16[128,256]{1,0:T(8,128)(2,1)} %c_ref.1, ...), custom_call_target="tpu_custom_call" | custom-call | tf_op jit(solution)/shard_map/pallas_call | solution.py:369
  46.6 1.9 %copy.13 = f32[64,2048]{1,0:T(8,128)} copy(f32[64,2048]{1,0:T(8,128)} %shard_map.100) | data formatting | bytes 1048576

commit v2 on v1

--- a/solution.py
+++ b/solution.py
@@ -27,9 +27,9 @@
     return lax.dot_general(a, b, dims, precision=precision, preferred_element_type=F32)
 
 
-def dot_nt(a, b):
+def dot_nt(a, b, precision=None):
     dims = (((1,), (1,)), ((), ()))
-    return lax.dot_general(a, b, dims, preferred_element_type=F32)
+    return lax.dot_general(a, b, dims, precision=precision, preferred_element_type=F32)
 
 
 def quarter_starts(width):
@@ -40,11 +40,11 @@
 def kernel(
     n, tp, heads, nq,
     q_ref, k_ref, v_ref, x_ref, gate_ref, b_ref, c_ref, rate_ref, wa_hbm, ws_hbm,
-    out_ref,
-    wa, ws, kv, bc, xs, xr, ds, dr, loc, tot, er, es, ysend, yrecv, psend, precv,
+    out_ref, precv,
+    wa, ws, kv, bc, xs, xr, ds, dr, loc, tot, er, es, ysend, yrecv, psend,
     qs, attn, yacc, grow, part, ssm, acc, peak, norm,
     wsem, swap_s, swap_r, col_s, col_r, pl_s, pl_r, bc_s, bc_r, x_s, x_r, d_s, d_r,
-    e_s, e_r, y_s, y_r, p_s, p_r,
+    e_s, e_r, y_s, y_r, p_s, p_r, o_s,
 ):
     s = lax.axis_index("seq")
     t = lax.axis_index("tp")
@@ -73,8 +73,11 @@
     for w in w_copies:
         w.start()
 
-    plane_peers = [z * PLANE + (i + d) % PLANE for d in range(1, PLANE)]
-    plane_index = [(i + d) % PLANE for d in range(1, PLANE)]
+    sib = i + 1 - 2 * (i % 2)
+    ynb = (i + 2) % PLANE
+    dia = (sib + 2) % PLANE
+    plane_index = [ynb, dia, sib]
+    plane_peers = [z * PLANE + j for j in plane_index]
     tp_peers = [(t + d) % tp for d in range(1, tp)]
     col_peers = [((z + d) % planes) * PLANE + i for d in range(1, planes)]
 
@@ -103,16 +106,18 @@
     for m, ref in enumerate((k_ref, v_ref)):
         kv[s, m, own_rows(t), :] = ref[:, kv_cols(t)]
 
-    bc_copies = []
-    for d, p in enumerate(plane_peers):
-        for m, ref in enumerate((b_ref, c_ref)):
-            bc_copies.append(copy(
-                ref, bc.at[i, m], bc_s.at[m, d], bc_r.at[m, d], (p, t)
-            ))
-    for c in bc_copies:
-        c.start()
+    def relay(ref_of, send, recv):
+        def move(block, kind, to):
+            ref = ref_of(block)
+            return copy(ref, ref, send.at[kind], recv.at[kind], (z * PLANE + to, t))
+        return [move(i, 0, sib), move(i, 1, ynb), move(ynb, 2, sib)]
+
     bc[i, 0] = b_ref[...]
     bc[i, 1] = c_ref[...]
+    b_moves = relay(lambda j: bc.at[j, 0], bc_s.at[0], bc_r.at[0])
+    c_moves = relay(lambda j: bc.at[j, 1], bc_s.at[1], bc_r.at[1])
+    b_moves[1].start()
+    b_moves[0].start()
 
     row_id = lax.broadcasted_iota(jnp.int32, (rows, rows), 0)
     col_id = lax.broadcasted_iota(jnp.int32, (rows, rows), 1)
@@ -120,8 +125,8 @@
     lower = jnp.where(causal, 1.0, 0.0).astype(F32)
     upper = jnp.where(row_id <= col_id, 1.0, 0.0).astype(F32)
     rates = -rate_ref[...]
-    cum = jnp.dot(lower, rates, precision=PRECISE, preferred_element_type=F32)
-    cum_t = dot_tn(rates, upper, PRECISE)
+    cum_t = jnp.dot(rates, upper, precision=PRECISE, preferred_element_type=F32)
+    cum = dot_nt(lower, rates, PRECISE)
     last = cum[rows - 1:rows, :]
     to_end = jnp.exp(last - cum)
     from_start = jnp.exp(cum)
@@ -153,18 +158,18 @@
         ))
     for c in x_copies:
         c.start()
+    c_moves[1].start()
+    c_moves[0].start()
+    b_moves[1].wait_recv()
+    b_moves[2].start()
     xr[i] = xs[i]
     dr[i] = ds[i]
 
     for c in swaps:
         c.wait_recv()
 
-    def to_plane(block):
-        src = kv.at[block * PLANE + i]
-        return [
-            copy(src, src, pl_s.at[block, d], pl_r.at[block, d], (p, t))
-            for d, p in enumerate(plane_peers)
-        ]
+    def kv_moves(zz):
+        return relay(lambda j: kv.at[zz * PLANE + j], pl_s.at[zz], pl_r.at[zz])
 
     def up(zz):
         src = kv.at[s]
@@ -178,7 +183,7 @@
     def _(zz):
         up(zz).start()
 
-    for c in to_plane(z):
+    for c in kv_moves(z)[:2]:
         c.start()
 
     read_write = dot_nt(c_ref[...], b_ref[...])
@@ -196,19 +201,19 @@
         yacc[:, cc] = dot(jnp.concatenate(factors, axis=1), stacked)
         grow[:, cc] = pair_cols(from_start, pair)
 
-    for c in bc_copies + x_copies:
+    c_moves[1].wait_recv()
+    c_moves[2].start()
+    for c in [b_moves[0], b_moves[2]] + x_copies:
         c.wait_recv()
-    for c in range(nch):
-        cc = slice(128 * c, 128 * (c + 1))
-        total = jnp.zeros((bc.shape[3], 128), F32)
-        decay = jnp.ones((1, 128), F32)
-        for j in range(PLANE):
-            block = dot_tn(bc[j, 0], xr[j, :, cc])
-            loc[j, :, cc] = block
-            total = dr[j, 0:1, cc] * total + block
-            decay = decay * dr[j, 0:1, cc]
-        tot[0, :, cc] = total
-        dr[PLANE, :, cc] = jnp.broadcast_to(decay, (8, 128))
+    total = jnp.zeros((bc.shape[3], span), F32)
+    decay = jnp.ones((1, span), F32)
+    for j in range(PLANE):
+        block = dot_tn(bc[j, 0], xr[j])
+        loc[j] = block
+        total = dr[j, 0:1, :] * total + block
+        decay = decay * dr[j, 0:1, :]
+    tot[0] = total
+    dr[PLANE] = jnp.broadcast_to(decay, (8, span))
 
     def chain(c):
         to = (jnp.minimum(z + 1, planes - 1) * PLANE + i, t)
@@ -221,36 +226,20 @@
     @pl.loop(0, z)
     def _(zz):
         col_from(zz).wait_recv()
-        for c in to_plane(zz):
+        for c in kv_moves(zz)[:2]:
             c.start()
 
-    for c in range(nch):
-        cc = slice(128 * c, 128 * (c + 1))
-
-        @pl.when(z > 0)
-        def _():
-            chain(c).wait_recv()
-
-        @pl.when(z < planes - 1)
-        def _():
-            entering = er[c].astype(F32)
-            es[c] = (dr[PLANE, 0:1, cc] * entering + tot[0, :, cc]).astype(BF16)
+    @pl.when(z == 0)
+    def _():
+        for c in range(nch):
+            es[c] = tot[0, :, 128 * c:128 * (c + 1)].astype(BF16)
             chain(c).start()
 
-    for c in range(nch):
-        cc = slice(128 * c, 128 * (c + 1))
-        state = er[c].astype(F32)
-        for j in range(PLANE):
-            ysend[j, :, cc] = dot(bc[j, 1], state.astype(BF16)).astype(BF16)
-            if j < PLANE - 1:
-                state = dr[j, 0:1, cc] * state + loc[j, :, cc]
-    y_copies = [
-        copy(ysend.at[plane_index[d]], yrecv.at[i], y_s.at[d], y_r.at[d], (p, t))
-        for d, p in enumerate(plane_peers)
-    ]
-    for c in y_copies:
-        c.start()
-    yrecv[i] = ysend[i]
+    @pl.loop(0, z + 1)
+    def _(zz):
+        moves = kv_moves(zz)
+        moves[1].wait_recv()
+        moves[2].start()
 
     for h in range(nq):
         lo = pl.multiple_of((t * nq + h) * HEAD, HEAD)
@@ -263,8 +252,9 @@
     wide = PLANE * rows
 
     def attend(zz, masked):
-        for c in to_plane(zz):
-            c.wait_recv()
+        moves = kv_moves(zz)
+        moves[0].wait_recv()
+        moves[2].wait_recv()
         keys = kv[pl.ds(zz * PLANE, PLANE), 0].reshape(wide, HEAD)
         vals = kv[pl.ds(zz * PLANE, PLANE), 1].reshape(wide, HEAD)
         for h in range(nq):
@@ -282,9 +272,45 @@
             acc[hh, :] = acc[hh, :] * shrink + dot(weights.astype(BF16), vals)
             peak[hh, 0:1] = new
 
+    early = z // 2 + (z // (planes - 1)) * (z - z // 2)
+
+    @pl.loop(0, early)
+    def _(zz):
+        attend(zz, False)
+
+    for c in range(nch):
+        cc = slice(128 * c, 128 * (c + 1))
+
+        @pl.when(z > 0)
+        def _():
+            chain(c).wait_recv()
+
+        @pl.when((z > 0) & (z < planes - 1))
+        def _():
+            entering = er[c].astype(F32)
+            es[c] = (dr[PLANE, 0:1, cc] * entering + tot[0, :, cc]).astype(BF16)
+            chain(c).start()
+
+    c_moves[0].wait_recv()
+    c_moves[2].wait_recv()
+    for c in range(nch):
+        cc = slice(128 * c, 128 * (c + 1))
+        state = er[c].astype(F32)
+        for j in range(PLANE):
+            ysend[j, :, cc] = dot(bc[j, 1], state.astype(BF16)).astype(BF16)
+            if j < PLANE - 1:
+                state = dr[j, 0:1, cc] * state + loc[j, :, cc]
+    y_copies = [
+        copy(ysend.at[plane_index[d]], yrecv.at[i], y_s.at[d], y_r.at[d], (p, t))
+        for d, p in enumerate(plane_peers)
+    ]
+    for c in y_copies:
+        c.start()
+    yrecv[i] = ysend[i]
+
     attend(z, True)
 
-    @pl.loop(0, z)
+    @pl.loop(early, z)
     def _(zz):
         attend(zz, False)
 
@@ -314,21 +340,18 @@
         psend[k] = value.astype(BF16)
         for d, p in enumerate(tp_peers):
             c = copy(
-                psend.at[k, own_rows(p)], precv.at[d, k],
+                psend.at[k, own_rows(p)], precv.at[d, :, k * cols:(k + 1) * cols],
                 p_s.at[d, k], p_r.at[d, k], (s, p),
             )
             c.start()
             p_copies.append((d, k, c))
-    for k in range(ncol):
-        cc = slice(k * cols, (k + 1) * cols)
-        value = part[own_rows(t), cc]
-        for d, kk, c in p_copies:
-            if kk == k:
-                c.wait_recv()
-                value = value + precv[d, k].astype(F32)
-        out_ref[:, cc] = value
-
-    for c in swaps + bc_copies + x_copies + y_copies + [c for _, _, c in p_copies]:
+    keep = pltpu.make_async_copy(part.at[own_rows(t)], out_ref, o_s)
+    keep.start()
+    for _, _, c in p_copies:
+        c.wait_recv()
+    keep.wait()
+
+    for c in swaps + b_moves + c_moves + x_copies + y_copies + [c for _, _, c in p_copies]:
         c.wait_send()
 
     @pl.loop(z + 1, planes)
@@ -337,7 +360,7 @@
 
     @pl.loop(0, z + 1)
     def _(zz):
-        for c in to_plane(zz):
+        for c in kv_moves(zz):
             c.wait_send()
 
     @pl.when(z < planes - 1)
@@ -366,12 +389,15 @@
     peers = PLANE - 1
     vmem = pltpu.VMEM
     dma = pltpu.SemaphoreType.DMA
-    return pl.pallas_call(
+    mine, others = pl.pallas_call(
         functools.partial(kernel, n, tp, heads, nq),
-        out_shape=jax.ShapeDtypeStruct((own, model), F32),
+        out_shape=(
+            jax.ShapeDtypeStruct((own, model), F32),
+            jax.ShapeDtypeStruct((tp - 1, own, model), BF16),
+        ),
         in_specs=[pl.BlockSpec(memory_space=pltpu.VMEM)] * 8
         + [pl.BlockSpec(memory_space=pl.ANY)] * 2,
-        out_specs=pl.BlockSpec(memory_space=pltpu.VMEM),
+        out_specs=(pl.BlockSpec(memory_space=pl.ANY),) * 2,
         scratch_shapes=[
             vmem(attn_out_weight.shape, BF16),
             vmem(ssm_out_weight.shape, BF16),
@@ -388,7 +414,6 @@
             vmem((PLANE, rows, span), BF16),
             vmem((PLANE, rows, span), BF16),
             vmem((ncol, rows, cols), BF16),
-            vmem((tp - 1, ncol, own, cols), BF16),
             vmem((nq * rows, HEAD), BF16),
             vmem((rows, nq * HEAD), BF16),
             vmem((rows, width), F32),
@@ -417,14 +442,18 @@
             dma((peers,)),
             dma((tp - 1, ncol)),
             dma((tp - 1, ncol)),
+            dma,
         ],
         compiler_params=pltpu.CompilerParams(
             collective_id=0, has_side_effects=True, vmem_limit_bytes=56 * 1024 * 1024
         ),
     )(
         queries, key_rows, value_rows, ssm_input, gate_input, write_vectors, read_vectors,
-        decay_rates, attn_out_weight, ssm_out_weight,
+        decay_rates.T, attn_out_weight, ssm_out_weight,
     )
+    for d in range(tp - 1):
+        mine = mine + others[d].astype(F32)
+    return mine
 
 
 def solution(mesh):

time: 48.7 us -> 41.5 us (0.85)
  Pallas kernels: 45.2 us -> 39.1 us
  local copies, waits for them, and re-layouts: 3.31 us -> 0 us
  other arithmetic: 0 us -> 1.95 us
    pallas_call x1, Pallas kernels: 45.2 us -> 39.1 us  [local(): pl.pallas_call(functools.partial(kernel, n, tp, heads, nq), out_shape=(ja...]
    unnamed x2 -> x0, local copies, waits for them, and re-layouts: 3.31 us -> none
    add x0 -> x1, other arithmetic: none -> 1.95 us  [local(): mine = mine + others[d].astype(F32)]
where the time goes in v2:
time: 41.5 us; the launch traced here: 41.1 us
  Pallas kernels  39.1 us (94%)
  other arithmetic  1.95 us (5%)
    pallas_call x1, Pallas kernels, local(): pl.pallas_call(functools.partial(kernel, n, tp, heads, nq), out_shape=(ja...  39.1 us
    add x1, other arithmetic, local(): mine = mine + others[d].astype(F32)  1.95 us

profile of v2, /device:TPU:24, one launch (start us, length us, event | category | flops | bytes accessed | tf_op | source)
XLA Modules:
  0.0 41.1 jit_solution(12702815714518199013)
XLA Ops:
  0.0 39.1 %shard_map.100 = (f32[64,2048]{1,0:T(8,128)}, bf16[1,64,2048]{2,1,0:T(8,128)(2,1)}) custom-call(bf16[128,1024]{1,0:T(8,128)(2,1)} %q_ref.1, bf16[64,256]{1,0:T(8,128)(2,1)} %k_ref.1, bf16[64,256]{1,0:T(8,128)(2,1)} %v_ref.1, bf16[128,1536]{1,0:T(8,128)(2,1)} %x_ref.1, bf16[128,1536]{1,0:T(8,128)(2,1)} %gate_ref.1, bf16[128,256]{1,0:T(8,128)(2,1)} %b_ref.1, ...), custom_call_target="tpu_custom_call" | custom-call | tf_op jit(solution)/shard_map/pallas_call | solution.py:392
  39.1 1.9 %convert_add_fusion = f32[64,2048]{1,0:T(8,128)} fusion(f32[64,2048]{1,0:T(8,128)} %get-tuple-element.7, bf16[1,64,2048]{2,1,0:T(8,128)(2,1)} %get-tuple-element.8), kind=kLoop, calls=%fused_computation | loop fusion | flops 262144 | bytes 1310720 | tf_op jit(solution)/shard_map/add | solution.py:455

commit v3 on v2

--- a/solution.py
+++ b/solution.py
@@ -41,7 +41,7 @@
     n, tp, heads, nq,
     q_ref, k_ref, v_ref, x_ref, gate_ref, b_ref, c_ref, rate_ref, wa_hbm, ws_hbm,
     out_ref, precv,
-    wa, ws, kv, bc, xs, xr, ds, dr, loc, tot, er, es, ysend, yrecv, psend,
+    wa, ws, kv, bc, xr, rr, grown, dr, loc, tot, er, es, ysend, yrecv, psend,
     qs, attn, yacc, grow, part, ssm, acc, peak, norm,
     wsem, swap_s, swap_r, col_s, col_r, pl_s, pl_r, bc_s, bc_r, x_s, x_r, d_s, d_r,
     e_s, e_r, y_s, y_r, p_s, p_r, o_s,
@@ -66,9 +66,22 @@
             device_id=to, device_id_type=MESH,
         )
 
-    w_copies = [
-        pltpu.make_async_copy(wa_hbm, wa, wsem.at[0]),
-        pltpu.make_async_copy(ws_hbm, ws, wsem.at[1]),
+    tiles = []
+    for c in range(nch):
+        seen = [lo for step in tiles for _, lo in step]
+        step = []
+        for q in range(PLANE):
+            lo = starts[q] + 128 * c
+            if lo not in seen:
+                step.append((q, lo))
+                seen.append(lo)
+        tiles.append(step)
+    order = [lo for step in tiles for _, lo in step]
+    w_copies = [pltpu.make_async_copy(wa_hbm, wa, wsem.at[len(order)])] + [
+        pltpu.make_async_copy(
+            ws_hbm.at[pl.ds(lo, 128)], ws.at[pl.ds(128 * k, 128)], wsem.at[k]
+        )
+        for k, lo in enumerate(order)
     ]
     for w in w_copies:
         w.start()
@@ -87,6 +100,37 @@
     for p in tp_peers:
         pl.semaphore_signal(barrier, inc=1, device_id=(s, p), device_id_type=MESH)
     pl.semaphore_wait(barrier, len(plane_peers) + len(col_peers) + len(tp_peers))
+
+    def relay(ref_of, send, recv):
+        def move(block, kind, to):
+            ref = ref_of(block)
+            return copy(ref, ref, send.at[kind], recv.at[kind], (z * PLANE + to, t))
+        return [move(i, 0, sib), move(i, 1, ynb), move(ynb, 2, sib)]
+
+    bc[i, 0] = b_ref[...]
+    bc[i, 1] = c_ref[...]
+    b_moves = relay(lambda j: bc.at[j, 0], bc_s.at[0], bc_r.at[0])
+    c_moves = relay(lambda j: bc.at[j, 1], bc_s.at[1], bc_r.at[1])
+    b_moves[1].start()
+    b_moves[0].start()
+
+    def quarter(q):
+        return pl.ds(pl.multiple_of(jnp.minimum(q * span, width - span), 128), span)
+
+    r_copies = [
+        copy(rate_ref, rr.at[i], d_s.at[d], d_r.at[d], (p, t))
+        for d, p in enumerate(plane_peers)
+    ]
+    x_copies = [
+        copy(x_ref.at[:, quarter(plane_index[d])], xr.at[i], x_s.at[d], x_r.at[d], (p, t))
+        for d, p in enumerate(plane_peers)
+    ]
+    for c in r_copies + x_copies:
+        c.start()
+    c_moves[1].start()
+    c_moves[0].start()
+    xr[i] = x_ref[:, quarter(i)]
+    rr[i] = rate_ref[...]
 
     def kv_cols(peer):
         return pl.ds(pl.multiple_of(peer * KVHEADS // tp * HEAD, HEAD), HEAD)
@@ -106,19 +150,6 @@
     for m, ref in enumerate((k_ref, v_ref)):
         kv[s, m, own_rows(t), :] = ref[:, kv_cols(t)]
 
-    def relay(ref_of, send, recv):
-        def move(block, kind, to):
-            ref = ref_of(block)
-            return copy(ref, ref, send.at[kind], recv.at[kind], (z * PLANE + to, t))
-        return [move(i, 0, sib), move(i, 1, ynb), move(ynb, 2, sib)]
-
-    bc[i, 0] = b_ref[...]
-    bc[i, 1] = c_ref[...]
-    b_moves = relay(lambda j: bc.at[j, 0], bc_s.at[0], bc_r.at[0])
-    c_moves = relay(lambda j: bc.at[j, 1], bc_s.at[1], bc_r.at[1])
-    b_moves[1].start()
-    b_moves[0].start()
-
     row_id = lax.broadcasted_iota(jnp.int32, (rows, rows), 0)
     col_id = lax.broadcasted_iota(jnp.int32, (rows, rows), 1)
     causal = row_id >= col_id
@@ -127,43 +158,13 @@
     rates = -rate_ref[...]
     cum_t = jnp.dot(rates, upper, precision=PRECISE, preferred_element_type=F32)
     cum = dot_nt(lower, rates, PRECISE)
-    last = cum[rows - 1:rows, :]
-    to_end = jnp.exp(last - cum)
     from_start = jnp.exp(cum)
-    whole_decay = jnp.exp(last)
     first_half = lax.broadcasted_iota(jnp.int32, (rows, 128), 1) < HDIM
-    first_half_8 = lax.broadcasted_iota(jnp.int32, (8, 128), 1) < HDIM
 
     def pair_cols(value, pair):
         a = value[:, 2 * pair:2 * pair + 1]
         b = value[:, 2 * pair + 1:2 * pair + 2]
-        mask = first_half if value.shape[0] == rows else first_half_8
-        return jnp.where(mask, a, b)
-
-    for q in range(PLANE):
-        for c in range(nch):
-            lo = starts[q] + 128 * c
-            pair = lo // 128
-            x = x_ref[:, lo:lo + 128].astype(F32)
-            xs[q, :, 128 * c:128 * (c + 1)] = (x * pair_cols(to_end, pair)).astype(BF16)
-            ds[q, :, 128 * c:128 * (c + 1)] = pair_cols(whole_decay, pair)
-
-    x_copies = []
-    for d, p in enumerate(plane_peers):
-        x_copies.append(copy(
-            xs.at[plane_index[d]], xr.at[i], x_s.at[d], x_r.at[d], (p, t)
-        ))
-        x_copies.append(copy(
-            ds.at[plane_index[d]], dr.at[i], d_s.at[d], d_r.at[d], (p, t)
-        ))
-    for c in x_copies:
-        c.start()
-    c_moves[1].start()
-    c_moves[0].start()
-    b_moves[1].wait_recv()
-    b_moves[2].start()
-    xr[i] = xs[i]
-    dr[i] = ds[i]
+        return jnp.where(first_half, a, b)
 
     for c in swaps:
         c.wait_recv()
@@ -185,6 +186,9 @@
 
     for c in kv_moves(z)[:2]:
         c.start()
+
+    b_moves[1].wait_recv()
+    b_moves[2].start()
 
     read_write = dot_nt(c_ref[...], b_ref[...])
     for pair in range(width // 128):
@@ -201,6 +205,18 @@
         yacc[:, cc] = dot(jnp.concatenate(factors, axis=1), stacked)
         grow[:, cc] = pair_cols(from_start, pair)
 
+    for c in r_copies:
+        c.wait_recv()
+    channel = lax.broadcasted_iota(jnp.int32, (heads, span), 1)
+    head = (channel + jnp.minimum(i * span, width - span)) // HDIM
+    pick = (lax.broadcasted_iota(jnp.int32, (heads, span), 0) == head).astype(F32)
+    for j in range(PLANE):
+        sums = dot_nt(lower, -rr[j], PRECISE)
+        end = sums[rows - 1:rows, :]
+        to_end = jnp.exp(end - sums)
+        grown[j] = jnp.dot(to_end, pick, precision=PRECISE, preferred_element_type=F32)
+        ends = jnp.broadcast_to(jnp.exp(end), (8, heads))
+        dr[j] = jnp.dot(ends, pick, precision=PRECISE, preferred_element_type=F32)
     c_moves[1].wait_recv()
     c_moves[2].start()
     for c in [b_moves[0], b_moves[2]] + x_copies:
@@ -208,7 +224,8 @@
     total = jnp.zeros((bc.shape[3], span), F32)
     decay = jnp.ones((1, span), F32)
     for j in range(PLANE):
-        block = dot_tn(bc[j, 0], xr[j])
+        scaled = (xr[j].astype(F32) * grown[j]).astype(BF16)
+        block = dot_tn(bc[j, 0], scaled)
         loc[j] = block
         total = dr[j, 0:1, :] * total + block
         decay = decay * dr[j, 0:1, :]
@@ -278,6 +295,9 @@
     def _(zz):
         attend(zz, False)
 
+    c_moves[0].wait_recv()
+    c_moves[2].wait_recv()
+    y_copies = []
     for c in range(nch):
         cc = slice(128 * c, 128 * (c + 1))
 
@@ -291,22 +311,19 @@
             es[c] = (dr[PLANE, 0:1, cc] * entering + tot[0, :, cc]).astype(BF16)
             chain(c).start()
 
-    c_moves[0].wait_recv()
-    c_moves[2].wait_recv()
-    for c in range(nch):
-        cc = slice(128 * c, 128 * (c + 1))
         state = er[c].astype(F32)
         for j in range(PLANE):
-            ysend[j, :, cc] = dot(bc[j, 1], state.astype(BF16)).astype(BF16)
+            ysend[c, j] = dot(bc[j, 1], state.astype(BF16)).astype(BF16)
             if j < PLANE - 1:
                 state = dr[j, 0:1, cc] * state + loc[j, :, cc]
-    y_copies = [
-        copy(ysend.at[plane_index[d]], yrecv.at[i], y_s.at[d], y_r.at[d], (p, t))
-        for d, p in enumerate(plane_peers)
-    ]
-    for c in y_copies:
-        c.start()
-    yrecv[i] = ysend[i]
+        sends = [
+            copy(ysend.at[c, plane_index[d]], yrecv.at[c, i], y_s.at[c, d], y_r.at[c, d], (p, t))
+            for d, p in enumerate(plane_peers)
+        ]
+        for m in sends:
+            m.start()
+        y_copies.append(sends)
+        yrecv[c, i] = ysend[c, i]
 
     attend(z, True)
 
@@ -323,35 +340,40 @@
         cc = slice(k * cols, (k + 1) * cols)
         part[:, cc] = dot(attn[...], wa[:, cc])
 
-    for c in y_copies:
-        c.wait_recv()
-    for q in range(PLANE):
-        for c in range(nch):
-            lo = starts[q] + 128 * c
+    p_copies = []
+    done = 0
+    for step in range(nch):
+        for m in y_copies[step]:
+            m.wait_recv()
+        depth = 128 * len(tiles[step])
+        for k, (q, lo) in enumerate(tiles[step]):
             cc = slice(lo, lo + 128)
             g = gate_ref[:, cc].astype(F32)
-            raw = yacc[:, cc] + grow[:, cc] * yrecv[q, :, 128 * c:128 * (c + 1)].astype(F32)
-            ssm[:, cc] = (raw * (g / (1.0 + jnp.exp(-g)))).astype(BF16)
-    p_copies = []
-    for k in range(ncol):
-        cc = slice(k * cols, (k + 1) * cols)
-        value = part[:, cc] + dot(ssm[...], ws[:, cc])
-        part[:, cc] = value
-        psend[k] = value.astype(BF16)
-        for d, p in enumerate(tp_peers):
-            c = copy(
-                psend.at[k, own_rows(p)], precv.at[d, :, k * cols:(k + 1) * cols],
-                p_s.at[d, k], p_r.at[d, k], (s, p),
-            )
-            c.start()
-            p_copies.append((d, k, c))
+            raw = yacc[:, cc] + grow[:, cc] * yrecv[step, q].astype(F32)
+            at = done + 128 * k
+            ssm[:, at:at + 128] = (raw * (g / (1.0 + jnp.exp(-g)))).astype(BF16)
+        for k in range(ncol):
+            cc = slice(k * cols, (k + 1) * cols)
+            value = part[:, cc] + dot(ssm[:, done:done + depth], ws[done:done + depth, cc])
+            part[:, cc] = value
+            if step == nch - 1:
+                psend[k] = value.astype(BF16)
+                for d, p in enumerate(tp_peers):
+                    c = copy(
+                        psend.at[k, own_rows(p)], precv.at[d, :, k * cols:(k + 1) * cols],
+                        p_s.at[d, k], p_r.at[d, k], (s, p),
+                    )
+                    c.start()
+                    p_copies.append((d, k, c))
+        done += depth
     keep = pltpu.make_async_copy(part.at[own_rows(t)], out_ref, o_s)
     keep.start()
     for _, _, c in p_copies:
         c.wait_recv()
     keep.wait()
 
-    for c in swaps + b_moves + c_moves + x_copies + y_copies + [c for _, _, c in p_copies]:
+    moved = swaps + b_moves + c_moves + r_copies + x_copies + sum(y_copies, [])
+    for c in moved + [c for _, _, c in p_copies]:
         c.wait_send()
 
     @pl.loop(z + 1, planes)
@@ -404,15 +426,15 @@
             vmem((n, 2, rows, HEAD), BF16),
             vmem((PLANE, 2, rows, state), BF16),
             vmem((PLANE, rows, span), BF16),
-            vmem((PLANE, rows, span), BF16),
-            vmem((PLANE, 8, span), F32),
+            vmem((PLANE, heads, rows), F32),
+            vmem((PLANE, rows, span), F32),
             vmem((PLANE + 1, 8, span), F32),
             vmem((PLANE, state, span), F32),
             vmem((1, state, span), F32),
             vmem((nch, state, 128), BF16),
             vmem((nch, state, 128), BF16),
-            vmem((PLANE, rows, span), BF16),
-            vmem((PLANE, rows, span), BF16),
+            vmem((nch, PLANE, rows, 128), BF16),
+            vmem((nch, PLANE, rows, 128), BF16),
             vmem((ncol, rows, cols), BF16),
             vmem((nq * rows, HEAD), BF16),
             vmem((rows, nq * HEAD), BF16),
@@ -423,7 +445,7 @@
             vmem((nq * rows, HEAD), F32),
             vmem((nq * rows, HEAD), F32),
             vmem((nq * rows, HEAD), F32),
-            dma((2,)),
+            dma((width // 128 + 1,)),
             dma((2, tp - 1)),
             dma((2, tp - 1)),
             dma((planes,)),
@@ -438,8 +460,8 @@
             dma((peers,)),
             dma((nch,)),
             dma((nch,)),
-            dma((peers,)),
-            dma((peers,)),
+            dma((nch, peers)),
+            dma((nch, peers)),
             dma((tp - 1, ncol)),
             dma((tp - 1, ncol)),
             dma,

time: 41.5 us -> 40 us (0.964)
  Pallas kernels: 39.1 us -> 37.9 us
    pallas_call x1, Pallas kernels: 39.1 us -> 37.9 us  [local(): pl.pallas_call(functools.partial(kernel, n, tp, heads, nq), out_shape=(ja...]
where the time goes in v3:
time: 40 us; the launch traced here: 39.9 us
  Pallas kernels  37.9 us (95%)
  other arithmetic  1.95 us (5%)
    pallas_call x1, Pallas kernels, local(): pl.pallas_call(functools.partial(kernel, n, tp, heads, nq), out_shape=(ja...  37.9 us
    add x1, other arithmetic, local(): mine = mine + others[d].astype(F32)  1.95 us

profile of v3, /device:TPU:24, one launch (start us, length us, event | category | flops | bytes accessed | tf_op | source)
XLA Modules:
  0.0 39.9 jit_solution(599428436232223135)
XLA Ops:
  0.0 37.9 %shard_map.100 = (f32[64,2048]{1,0:T(8,128)}, bf16[1,64,2048]{2,1,0:T(8,128)(2,1)}) custom-call(bf16[128,1024]{1,0:T(8,128)(2,1)} %q_ref.1, bf16[64,256]{1,0:T(8,128)(2,1)} %k_ref.1, bf16[64,256]{1,0:T(8,128)(2,1)} %v_ref.1, bf16[128,1536]{1,0:T(8,128)(2,1)} %x_ref.1, bf16[128,1536]{1,0:T(8,128)(2,1)} %gate_ref.1, bf16[128,256]{1,0:T(8,128)(2,1)} %b_ref.1, ...), custom_call_target="tpu_custom_call" | custom-call | tf_op jit(solution)/shard_map/pallas_call | solution.py:414
  37.9 1.9 %convert_add_fusion = f32[64,2048]{1,0:T(8,128)} fusion(f32[64,2048]{1,0:T(8,128)} %get-tuple-element.7, bf16[1,64,2048]{2,1,0:T(8,128)(2,1)} %get-tuple-element.8), kind=kLoop, calls=%fused_computation | loop fusion | flops 262144 | bytes 1310720 | tf_op jit(solution)/shard_map/add | solution.py:477

commit v4 on v3

--- a/solution.py
+++ b/solution.py
@@ -41,7 +41,7 @@
     n, tp, heads, nq,
     q_ref, k_ref, v_ref, x_ref, gate_ref, b_ref, c_ref, rate_ref, wa_hbm, ws_hbm,
     out_ref, precv,
-    wa, ws, kv, bc, xr, rr, grown, dr, loc, tot, er, es, ysend, yrecv, psend,
+    wa, ws, kv, bc, xr, rr, dr, loc, tot, er, es, ysend, yrecv, psend,
     qs, attn, yacc, grow, part, ssm, acc, peak, norm,
     wsem, swap_s, swap_r, col_s, col_r, pl_s, pl_r, bc_s, bc_r, x_s, x_r, d_s, d_r,
     e_s, e_r, y_s, y_r, p_s, p_r, o_s,
@@ -190,6 +190,61 @@
     b_moves[1].wait_recv()
     b_moves[2].start()
 
+    for c in r_copies:
+        c.wait_recv()
+    channel = lax.broadcasted_iota(jnp.int32, (PLANE * heads, span), 1)
+    head = (channel + jnp.minimum(i * span, width - span)) // HDIM
+    line = lax.broadcasted_iota(jnp.int32, (PLANE * heads, span), 0)
+    pick = jnp.concatenate(
+        [(line == head + j * heads).astype(F32) for j in range(PLANE)], axis=1
+    )
+    sums = dot_nt(lower, -jnp.concatenate([rr[j] for j in range(PLANE)], axis=0), PRECISE)
+    end = sums[rows - 1:rows, :]
+    ends = jnp.broadcast_to(jnp.exp(end), (8, PLANE * heads))
+    to_end = jnp.concatenate([jnp.exp(end - sums), ends], axis=0)
+    spread = jnp.dot(to_end, pick, precision=PRECISE, preferred_element_type=F32)
+    for j in range(PLANE):
+        dr[j] = spread[rows:, span * j:span * (j + 1)]
+    c_moves[1].wait_recv()
+    c_moves[2].start()
+    for c in [b_moves[0], b_moves[2]] + x_copies:
+        c.wait_recv()
+    total = jnp.zeros((bc.shape[3], span), F32)
+    decay = jnp.ones((1, span), F32)
+    for j in range(PLANE):
+        scaled = (xr[j].astype(F32) * spread[:rows, span * j:span * (j + 1)]).astype(BF16)
+        block = dot_tn(bc[j, 0], scaled)
+        loc[j] = block
+        total = dr[j, 0:1, :] * total + block
+        decay = decay * dr[j, 0:1, :]
+    tot[0] = total
+    dr[PLANE] = jnp.broadcast_to(decay, (8, span))
+
+    half = bc.shape[3] // 2
+    pieces = [(c, m) for c in range(nch) for m in range(2)]
+
+    def chain(c, m):
+        to = (jnp.minimum(z + 1, planes - 1) * PLANE + i, t)
+        ms = slice(half * m, half * (m + 1))
+        return copy(es.at[c, ms], er.at[c, ms], e_s.at[c, m], e_r.at[c, m], to)
+
+    @pl.when(z == 0)
+    def _():
+        er[...] = jnp.zeros_like(er)
+
+    @pl.when(z == 0)
+    def _():
+        for c, m in pieces:
+            ms = slice(half * m, half * (m + 1))
+            es[c, ms, :] = tot[0, ms, 128 * c:128 * (c + 1)].astype(BF16)
+            chain(c, m).start()
+
+    @pl.loop(0, z)
+    def _(zz):
+        col_from(zz).wait_recv()
+        for c in kv_moves(zz)[:2]:
+            c.start()
+
     read_write = dot_nt(c_ref[...], b_ref[...])
     for pair in range(width // 128):
         cc = slice(128 * pair, 128 * (pair + 1))
@@ -204,53 +259,6 @@
         )
         yacc[:, cc] = dot(jnp.concatenate(factors, axis=1), stacked)
         grow[:, cc] = pair_cols(from_start, pair)
-
-    for c in r_copies:
-        c.wait_recv()
-    channel = lax.broadcasted_iota(jnp.int32, (heads, span), 1)
-    head = (channel + jnp.minimum(i * span, width - span)) // HDIM
-    pick = (lax.broadcasted_iota(jnp.int32, (heads, span), 0) == head).astype(F32)
-    for j in range(PLANE):
-        sums = dot_nt(lower, -rr[j], PRECISE)
-        end = sums[rows - 1:rows, :]
-        to_end = jnp.exp(end - sums)
-        grown[j] = jnp.dot(to_end, pick, precision=PRECISE, preferred_element_type=F32)
-        ends = jnp.broadcast_to(jnp.exp(end), (8, heads))
-        dr[j] = jnp.dot(ends, pick, precision=PRECISE, preferred_element_type=F32)
-    c_moves[1].wait_recv()
-    c_moves[2].start()
-    for c in [b_moves[0], b_moves[2]] + x_copies:
-        c.wait_recv()
-    total = jnp.zeros((bc.shape[3], span), F32)
-    decay = jnp.ones((1, span), F32)
-    for j in range(PLANE):
-        scaled = (xr[j].astype(F32) * grown[j]).astype(BF16)
-        block = dot_tn(bc[j, 0], scaled)
-        loc[j] = block
-        total = dr[j, 0:1, :] * total + block
-        decay = decay * dr[j, 0:1, :]
-    tot[0] = total
-    dr[PLANE] = jnp.broadcast_to(decay, (8, span))
-
-    def chain(c):
-        to = (jnp.minimum(z + 1, planes - 1) * PLANE + i, t)
-        return copy(es.at[c], er.at[c], e_s.at[c], e_r.at[c], to)
-
-    @pl.when(z == 0)
-    def _():
-        er[...] = jnp.zeros_like(er)
-
-    @pl.loop(0, z)
-    def _(zz):
-        col_from(zz).wait_recv()
-        for c in kv_moves(zz)[:2]:
-            c.start()
-
-    @pl.when(z == 0)
-    def _():
-        for c in range(nch):
-            es[c] = tot[0, :, 128 * c:128 * (c + 1)].astype(BF16)
-            chain(c).start()
 
     @pl.loop(0, z + 1)
     def _(zz):
@@ -298,18 +306,24 @@
     c_moves[0].wait_recv()
     c_moves[2].wait_recv()
     y_copies = []
+
+    @pl.when((z > 0) & (z < planes - 1))
+    def _():
+        for c, m in pieces:
+            cc = slice(128 * c, 128 * (c + 1))
+            ms = slice(half * m, half * (m + 1))
+            chain(c, m).wait_recv()
+            entering = er[c, ms, :].astype(F32)
+            es[c, ms, :] = (dr[PLANE, 0:1, cc] * entering + tot[0, ms, cc]).astype(BF16)
+            chain(c, m).start()
+
     for c in range(nch):
         cc = slice(128 * c, 128 * (c + 1))
 
-        @pl.when(z > 0)
+        @pl.when((z > 0) & (z == planes - 1))
         def _():
-            chain(c).wait_recv()
-
-        @pl.when((z > 0) & (z < planes - 1))
-        def _():
-            entering = er[c].astype(F32)
-            es[c] = (dr[PLANE, 0:1, cc] * entering + tot[0, :, cc]).astype(BF16)
-            chain(c).start()
+            for m in range(2):
+                chain(c, m).wait_recv()
 
         state = er[c].astype(F32)
         for j in range(PLANE):
@@ -387,8 +401,8 @@
 
     @pl.when(z < planes - 1)
     def _():
-        for c in range(nch):
-            chain(c).wait_send()
+        for c, m in pieces:
+            chain(c, m).wait_send()
 
 
 def local(
@@ -406,7 +420,7 @@
     own = rows // tp
     span, _ = quarter_starts(width)
     nch = span // 128
-    ncol = 4
+    ncol = 8
     cols = model // ncol
     peers = PLANE - 1
     vmem = pltpu.VMEM
@@ -427,7 +441,6 @@
             vmem((PLANE, 2, rows, state), BF16),
             vmem((PLANE, rows, span), BF16),
             vmem((PLANE, heads, rows), F32),
-            vmem((PLANE, rows, span), F32),
             vmem((PLANE + 1, 8, span), F32),
             vmem((PLANE, state, span), F32),
             vmem((1, state, span), F32),
@@ -458,8 +471,8 @@
             dma((peers,)),
             dma((peers,)),
             dma((peers,)),
-            dma((nch,)),
-            dma((nch,)),
+            dma((nch, 2)),
+            dma((nch, 2)),
             dma((nch, peers)),
             dma((nch, peers)),
             dma((tp - 1, ncol)),

time: 40 us -> 40.2 us (level)
  no operation moved by 1% of the time
where the time goes in v4:
time: 40.2 us; the launch traced here: 40 us
  Pallas kernels  38 us (95%)
  other arithmetic  1.95 us (5%)
    pallas_call x1, Pallas kernels, local(): pl.pallas_call(functools.partial(kernel, n, tp, heads, nq), out_shape=(ja...  38 us
    add x1, other arithmetic, local(): mine = mine + others[d].astype(F32)  1.95 us

profile of v4, /device:TPU:24, one launch (start us, length us, event | category | flops | bytes accessed | tf_op | source)
XLA Modules:
  0.0 40.0 jit_solution(18127341741396763386)
XLA Ops:
  0.0 38.0 %shard_map.100 = (f32[64,2048]{1,0:T(8,128)}, bf16[1,64,2048]{2,1,0:T(8,128)(2,1)}) custom-call(bf16[128,1024]{1,0:T(8,128)(2,1)} %q_ref.1, bf16[64,256]{1,0:T(8,128)(2,1)} %k_ref.1, bf16[64,256]{1,0:T(8,128)(2,1)} %v_ref.1, bf16[128,1536]{1,0:T(8,128)(2,1)} %x_ref.1, bf16[128,1536]{1,0:T(8,128)(2,1)} %gate_ref.1, bf16[128,256]{1,0:T(8,128)(2,1)} %b_ref.1, ...), custom_call_target="tpu_custom_call" | custom-call | tf_op jit(solution)/shard_map/pallas_call | solution.py:428
  38.0 1.9 %convert_add_fusion = f32[64,2048]{1,0:T(8,128)} fusion(f32[64,2048]{1,0:T(8,128)} %get-tuple-element.7, bf16[1,64,2048]{2,1,0:T(8,128)(2,1)} %get-tuple-element.8), kind=kLoop, calls=%fused_computation | loop fusion | flops 262144 | bytes 1310720 | tf_op jit(solution)/shard_map/add | solution.py:490

commit v5 on v4

--- a/solution.py
+++ b/solution.py
@@ -39,12 +39,13 @@
 
 def kernel(
     n, tp, heads, nq,
-    q_ref, k_ref, v_ref, x_ref, gate_ref, b_ref, c_ref, rate_ref, wa_hbm, ws_hbm,
+    q_in, k_in, v_in, x_in, gate_in, b_in, c_in, rate_in, wa_hbm, ws_hbm,
     out_ref, precv,
+    q_ref, k_ref, v_ref, x_ref, gate_ref, b_ref, c_ref, rate_ref,
     wa, ws, kv, bc, xr, rr, dr, loc, tot, er, es, ysend, yrecv, psend,
     qs, attn, yacc, grow, part, ssm, acc, peak, norm,
     wsem, swap_s, swap_r, col_s, col_r, pl_s, pl_r, bc_s, bc_r, x_s, x_r, d_s, d_r,
-    e_s, e_r, y_s, y_r, p_s, p_r, o_s,
+    e_s, e_r, y_s, y_r, p_s, p_r, o_s, in_s,
 ):
     s = lax.axis_index("seq")
     t = lax.axis_index("tp")
@@ -83,8 +84,15 @@
         )
         for k, lo in enumerate(order)
     ]
-    for w in w_copies:
-        w.start()
+    fetch = [
+        pltpu.make_async_copy(src, dst, in_s.at[k])
+        for k, (src, dst) in enumerate((
+            (b_in, b_ref), (rate_in, rate_ref), (x_in, x_ref), (c_in, c_ref),
+            (k_in, k_ref), (v_in, v_ref), (q_in, q_ref), (gate_in, gate_ref),
+        ))
+    ]
+    for c in fetch:
+        c.start()
 
     sib = i + 1 - 2 * (i % 2)
     ynb = (i + 2) % PLANE
@@ -99,6 +107,8 @@
         pl.semaphore_signal(barrier, inc=1, device_id=(p, t), device_id_type=MESH)
     for p in tp_peers:
         pl.semaphore_signal(barrier, inc=1, device_id=(s, p), device_id_type=MESH)
+    for c in fetch:
+        c.wait()
     pl.semaphore_wait(barrier, len(plane_peers) + len(col_peers) + len(tp_peers))
 
     def relay(ref_of, send, recv):
@@ -131,6 +141,9 @@
     c_moves[0].start()
     xr[i] = x_ref[:, quarter(i)]
     rr[i] = rate_ref[...]
+
+    for w in w_copies:
+        w.start()
 
     def kv_cols(peer):
         return pl.ds(pl.multiple_of(peer * KVHEADS // tp * HEAD, HEAD), HEAD)
@@ -405,6 +418,13 @@
             chain(c, m).wait_send()
 
 
+def add_shares(mine_ref, others_ref, out_ref):
+    total = mine_ref[...]
+    for d in range(others_ref.shape[0]):
+        total = total + others_ref[d].astype(F32)
+    out_ref[...] = total
+
+
 def local(
     n, tp,
     queries, key_rows, value_rows, ssm_input, gate_input, write_vectors, read_vectors,
@@ -431,10 +451,17 @@
             jax.ShapeDtypeStruct((own, model), F32),
             jax.ShapeDtypeStruct((tp - 1, own, model), BF16),
         ),
-        in_specs=[pl.BlockSpec(memory_space=pltpu.VMEM)] * 8
-        + [pl.BlockSpec(memory_space=pl.ANY)] * 2,
+        in_specs=[pl.BlockSpec(memory_space=pl.ANY)] * 10,
         out_specs=(pl.BlockSpec(memory_space=pl.ANY),) * 2,
         scratch_shapes=[
+            vmem(queries.shape, BF16),
+            vmem(key_rows.shape, BF16),
+            vmem(value_rows.shape, BF16),
+            vmem(ssm_input.shape, BF16),
+            vmem(gate_input.shape, BF16),
+            vmem(write_vectors.shape, BF16),
+            vmem(read_vectors.shape, BF16),
+            vmem((heads, rows), F32),
             vmem(attn_out_weight.shape, BF16),
             vmem(ssm_out_weight.shape, BF16),
             vmem((n, 2, rows, HEAD), BF16),
@@ -478,6 +505,7 @@
             dma((tp - 1, ncol)),
             dma((tp - 1, ncol)),
             dma,
+            dma((8,)),
         ],
         compiler_params=pltpu.CompilerParams(
             collective_id=0, has_side_effects=True, vmem_limit_bytes=56 * 1024 * 1024
@@ -486,9 +514,12 @@
         queries, key_rows, value_rows, ssm_input, gate_input, write_vectors, read_vectors,
         decay_rates.T, attn_out_weight, ssm_out_weight,
     )
-    for d in range(tp - 1):
-        mine = mine + others[d].astype(F32)
-    return mine
+    return pl.pallas_call(
+        add_shares,
+        out_shape=jax.ShapeDtypeStruct((own, model), F32),
+        in_specs=[pl.BlockSpec(memory_space=pltpu.VMEM)] * 2,
+        out_specs=pl.BlockSpec(memory_space=pltpu.VMEM),
+    )(mine, others)
 
 
 def solution(mesh):

time: 40.2 us -> 39.4 us (0.980)
  other arithmetic: 1.95 us -> 0 us
  Pallas kernels: 38 us -> 39.3 us
    add x1 -> x0, other arithmetic: 1.95 us -> none  [local(): mine = mine + others[d].astype(F32)]
    pallas_call x0 -> x1, Pallas kernels: none -> 1.95 us  [local(): pl.pallas_call(add_shares, out_shape=jax.ShapeDtypeStruct((own, model), F...]
    pallas_call x1, Pallas kernels: 38 us -> 37.3 us  [local(): pl.pallas_call(functools.partial(kernel, n, tp, heads, nq), out_shape=(ja...]
where the time goes in v5:
time: 39.4 us; the launch traced here: 39.3 us
  Pallas kernels  39.3 us (100%)
    pallas_call x1, Pallas kernels, local(): pl.pallas_call(functools.partial(kernel, n, tp, heads, nq), out_shape=(ja...  37.3 us
    pallas_call x1, Pallas kernels, local(): pl.pallas_call(add_shares, out_shape=jax.ShapeDtypeStruct((own, model), F...  1.95 us

profile of v5, /device:TPU:24, one launch (start us, length us, event | category | flops | bytes accessed | tf_op | source)
XLA Modules:
  0.0 39.3 jit_solution(13118673566389943032)
XLA Ops:
  0.0 37.3 %shard_map.100 = (f32[64,2048]{1,0:T(8,128)}, bf16[1,64,2048]{2,1,0:T(8,128)(2,1)}) custom-call(bf16[128,1024]{1,0:T(8,128)(2,1)} %q_in.1, bf16[64,256]{1,0:T(8,128)(2,1)} %k_in.1, bf16[64,256]{1,0:T(8,128)(2,1)} %v_in.1, bf16[128,1536]{1,0:T(8,128)(2,1)} %x_in.1, bf16[128,1536]{1,0:T(8,128)(2,1)} %gate_in.1, bf16[128,256]{1,0:T(8,128)(2,1)} %b_in.1, ...), custom_call_target="tpu_custom_call" | custom-call | tf_op jit(solution)/shard_map/pallas_call | solution.py:448
  37.3 1.9 %shard_map.101 = f32[64,2048]{1,0:T(8,128)} custom-call(f32[64,2048]{1,0:T(8,128)} %get-tuple-element.7.mine_ref, bf16[1,64,2048]{2,1,0:T(8,128)(2,1)} %get-tuple-element.8.others_ref), custom_call_target="tpu_custom_call" | custom-call | tf_op jit(solution)/shard_map/pallas_call | solution.py:517

commit v6 on v5

--- a/solution.py
+++ b/solution.py
@@ -289,7 +289,7 @@
     scale = 1.0 / math.sqrt(HEAD)
     wide = PLANE * rows
 
-    def attend(zz, masked):
+    def attend(zz):
         moves = kv_moves(zz)
         moves[0].wait_recv()
         moves[2].wait_recv()
@@ -298,10 +298,10 @@
         for h in range(nq):
             hh = slice(h * rows, (h + 1) * rows)
             scores = dot_nt(qs[hh, :], keys) * scale
-            if masked:
-                key_id = lax.broadcasted_iota(jnp.int32, (rows, wide), 1)
-                query_id = lax.broadcasted_iota(jnp.int32, (rows, wide), 0) + i * rows
-                scores = jnp.where(key_id <= query_id, scores, -1e30)
+            key_id = lax.broadcasted_iota(jnp.int32, (rows, wide), 1)
+            query_id = lax.broadcasted_iota(jnp.int32, (rows, wide), 0)
+            ahead = (z - zz) * wide + i * rows
+            scores = jnp.where(key_id <= query_id + ahead, scores, -1e30)
             old = peak[hh, 0:1]
             new = jnp.maximum(old, jnp.max(scores, axis=1, keepdims=True))
             weights = jnp.exp(scores - new)
@@ -310,11 +310,11 @@
             acc[hh, :] = acc[hh, :] * shrink + dot(weights.astype(BF16), vals)
             peak[hh, 0:1] = new
 
-    early = z // 2 + (z // (planes - 1)) * (z - z // 2)
+    early = z // 2 + (z // (planes - 1)) * (z + 1 - z // 2)
 
     @pl.loop(0, early)
     def _(zz):
-        attend(zz, False)
+        attend(zz)
 
     c_moves[0].wait_recv()
     c_moves[2].wait_recv()
@@ -352,11 +352,9 @@
         y_copies.append(sends)
         yrecv[c, i] = ysend[c, i]
 
-    attend(z, True)
-
-    @pl.loop(early, z)
-    def _(zz):
-        attend(zz, False)
+    @pl.loop(early, z + 1)
+    def _(zz):
+        attend(zz)
 
     for h in range(nq):
         hh = slice(h * rows, (h + 1) * rows)

time: 39.4 us -> 40.9 us (1.038)
  Pallas kernels: 39.3 us -> 40.7 us
    pallas_call x1, Pallas kernels: 37.3 us -> 38.8 us  [local(): pl.pallas_call(functools.partial(kernel, n, tp, heads, nq), out_shape=(ja...]
where the time goes in v6:
time: 40.9 us; the launch traced here: 40.8 us
  Pallas kernels  40.7 us (100%)
    pallas_call x1, Pallas kernels, local(): pl.pallas_call(functools.partial(kernel, n, tp, heads, nq), out_shape=(ja...  38.8 us
    pallas_call x1, Pallas kernels, local(): pl.pallas_call(add_shares, out_shape=jax.ShapeDtypeStruct((own, model), F...  1.95 us

profile of v6, /device:TPU:24, one launch (start us, length us, event | category | flops | bytes accessed | tf_op | source)
XLA Modules:
  0.0 40.8 jit_solution(16355539755370337309)
XLA Ops:
  0.0 38.8 %shard_map.100 = (f32[64,2048]{1,0:T(8,128)}, bf16[1,64,2048]{2,1,0:T(8,128)(2,1)}) custom-call(bf16[128,1024]{1,0:T(8,128)(2,1)} %q_in.1, bf16[64,256]{1,0:T(8,128)(2,1)} %k_in.1, bf16[64,256]{1,0:T(8,128)(2,1)} %v_in.1, bf16[128,1536]{1,0:T(8,128)(2,1)} %x_in.1, bf16[128,1536]{1,0:T(8,128)(2,1)} %gate_in.1, bf16[128,256]{1,0:T(8,128)(2,1)} %b_in.1, ...), custom_call_target="tpu_custom_call" | custom-call | tf_op jit(solution)/shard_map/pallas_call | solution.py:446
  38.8 1.9 %shard_map.101 = f32[64,2048]{1,0:T(8,128)} custom-call(f32[64,2048]{1,0:T(8,128)} %get-tuple-element.7.mine_ref, bf16[1,64,2048]{2,1,0:T(8,128)(2,1)} %get-tuple-element.8.others_ref), custom_call_target="tpu_custom_call" | custom-call | tf_op jit(solution)/shard_map/pallas_call | solution.py:515

commit v7 on v5

--- a/solution.py
+++ b/solution.py
@@ -310,7 +310,7 @@
             acc[hh, :] = acc[hh, :] * shrink + dot(weights.astype(BF16), vals)
             peak[hh, 0:1] = new
 
-    early = z // 2 + (z // (planes - 1)) * (z - z // 2)
+    early = z // 2
 
     @pl.loop(0, early)
     def _(zz):

time: 39.4 us -> 39.9 us (1.013)
  no operation moved by 1% of the time
where the time goes in v7:
time: 39.9 us; the launch traced here: 39.6 us
  Pallas kernels  39.6 us (99%)
    pallas_call x1, Pallas kernels, local(): pl.pallas_call(functools.partial(kernel, n, tp, heads, nq), out_shape=(ja...  37.7 us
    pallas_call x1, Pallas kernels, local(): pl.pallas_call(add_shares, out_shape=jax.ShapeDtypeStruct((own, model), F...  1.95 us

profile of v7, /device:TPU:24, one launch (start us, length us, event | category | flops | bytes accessed | tf_op | source)
XLA Modules:
  0.0 39.6 jit_solution(11568137931959477490)
XLA Ops:
  0.0 37.7 %shard_map.100 = (f32[64,2048]{1,0:T(8,128)}, bf16[1,64,2048]{2,1,0:T(8,128)(2,1)}) custom-call(bf16[128,1024]{1,0:T(8,128)(2,1)} %q_in.1, bf16[64,256]{1,0:T(8,128)(2,1)} %k_in.1, bf16[64,256]{1,0:T(8,128)(2,1)} %v_in.1, bf16[128,1536]{1,0:T(8,128)(2,1)} %x_in.1, bf16[128,1536]{1,0:T(8,128)(2,1)} %gate_in.1, bf16[128,256]{1,0:T(8,128)(2,1)} %b_in.1, ...), custom_call_target="tpu_custom_call" | custom-call | tf_op jit(solution)/shard_map/pallas_call | solution.py:448
  37.7 1.9 %shard_map.101 = f32[64,2048]{1,0:T(8,128)} custom-call(f32[64,2048]{1,0:T(8,128)} %get-tuple-element.7.mine_ref, bf16[1,64,2048]{2,1,0:T(8,128)(2,1)} %get-tuple-element.8.others_ref), custom_call_target="tpu_custom_call" | custom-call | tf_op jit(solution)/shard_map/pallas_call | solution.py:517
